TPU v7x, 32 devices: a whole 2x2x4 slice. The times are simulated.
32 devices in a mesh: section: 4 (over z), dp: 8 (over y, x, core).
Axes of the slice: x: 2, y: 2, z: 4, core: 2. Of those that a mesh axis runs over, the one named last changes fastest.
Arguments:
- tokens: int32 [32, 640], P('dp'), may hold values from 0 to 255
- padding_mask: int32 [32, 640], P('dp'), may hold values from 0 to 1, as said below
- embedding: float32 [512, 256], P('dp', 'section'), may hold values from -0.5 to 0.5
- mixer_weight: float32 [2, 512, 1536], P(None, 'dp'), may hold values from -0.25 to 0.25
- output_weight: float32 [2, 512, 512], P(None, 'dp'), may hold values from -0.75 to 0.75
- mixer_gain: float32 [2, 512], P(None, 'dp'), may hold values from 0.5 to 1.5
- expand_weight: float32 [2, 512, 2048], P(None, 'dp'), may hold values from -0.25 to 0.25
- reduce_weight: float32 [2, 2048, 512], P(None, 'dp'), may hold values from -0.125 to 0.125
- feed_gain: float32 [2, 512], P(None, 'dp'), may hold values from 0.5 to 1.5
- final_gain: float32 [512], P('dp'), may hold values from 0.5 to 1.5
Outputs:
- item_loss: float32 [32], P('dp')
- logit_grad: float32 [32, 640, 256], P('dp', None, 'section')
- embedding_grad: float32 [512, 256], P('dp', 'section')
- mixer_grad: float32 [2, 512, 1536], P(None, 'dp')
- output_grad: float32 [2, 512, 512], P(None, 'dp')
- mixer_gain_grad: float32 [2, 512], P(None, 'dp')
- expand_grad: float32 [2, 512, 2048], P(None, 'dp')
- reduce_grad: float32 [2, 2048, 512], P(None, 'dp')
- feed_gain_grad: float32 [2, 512], P(None, 'dp')
- final_gain_grad: float32 [512], P('dp')
Inputs may be any that keep to these rules, and one draw needn't show every extreme that they name: `padding_mask`: each item's mask is 1 on its first 320 or more positions and 0 on all positions after them.
All inputs are finite; a program needn't handle non-finite values.
Results may differ from a plain program's by a relative error of at most 0.006.
The roundings to bfloat16 on the way count: a program that leaves them out, or rounds other values in their place, can miss the bound.
Values may be sent and summed in bfloat16 or wider, within the bound.
A program may use at most 192 MiB of HBM per device.

v0:
```python
import jax
import jax.numpy as jnp
from jax import lax
from jax.sharding import PartitionSpec as P

D = 512
HEADS = 8
HD = 64
FF = 2048
VOCAB = 256
BAND = 30
MICRO = 4


def shifted_2(block, axis, distance):
    devices = range(lax.axis_size(axis))
    route = [(i - distance, i) for i in devices if i - distance in devices]
    return lax.ppermute(block, axis, route)


def spread(block, axis, source):
    block = jnp.where(lax.axis_index(axis) == source, block, jnp.zeros_like(block))
    return lax.psum(block, axis)


def product(left, right):
    return jnp.dot(left, right, preferred_element_type=jnp.float32)


def norm_scale(values, gain):
    return values * lax.rsqrt(jnp.mean(values * values, axis=-1, keepdims=True) + 1e-05) * gain


def head_mixture(scores, near_far, tanh_far, band_ok, causal, position):
    shifted = jnp.where(band_ok, 0.125 * scores, -1e30)
    largest = jnp.max(shifted, axis=-1, keepdims=True)
    weights = jnp.where(band_ok, jnp.exp(shifted - largest), 0.0)
    near = weights / jnp.sum(weights, axis=-1, keepdims=True)
    kept = jnp.where(causal, near_far, 0.0)
    first_far = kept / (jnp.sum(kept, axis=-1, keepdims=True) + 1.0)
    second_far = jnp.where(causal, tanh_far, 0.0) / (position + 1.0)
    return near + first_far + second_far


def features(head_query, head_key):
    return (
        jax.nn.elu(head_query) + 1.0,
        jax.nn.elu(head_key) + 1.0,
        jnp.tanh(head_query),
        jnp.tanh(head_key),
    )


def band_masks(length):
    row_index = lax.broadcasted_iota(jnp.int32, (length, length), 0)
    col_index = lax.broadcasted_iota(jnp.int32, (length, length), 1)
    causal = col_index <= row_index
    band_ok = causal & (row_index - col_index < BAND)
    return (causal, band_ok, row_index[:, :1].astype(jnp.float32))


def head_forward(triple):
    head_query, head_key, head_value = triple
    causal, band_ok, position = band_masks(head_query.shape[0])
    scores = product(head_query, head_key.T)
    mapped = features(head_query.astype(jnp.float32), head_key.astype(jnp.float32))
    first_query, first_key, second_query, second_key = [
        piece.astype(jnp.bfloat16) for piece in mapped
    ]
    near_far = product(first_query, first_key.T)
    tanh_far = product(second_query, second_key.T)
    mixture = head_mixture(scores, near_far, tanh_far, band_ok, causal, position).astype(
        jnp.bfloat16
    )
    return product(mixture, head_value).astype(jnp.bfloat16)


def head_backward(quad):
    head_query, head_key, head_value, grad_head = quad
    causal, band_ok, position = band_masks(head_query.shape[0])
    mapped, feature_pull = jax.vjp(
        features, head_query.astype(jnp.float32), head_key.astype(jnp.float32)
    )
    first_query, first_key, second_query, second_key = [
        piece.astype(jnp.bfloat16) for piece in mapped
    ]
    scores = product(head_query, head_key.T)
    near_far = product(first_query, first_key.T)
    tanh_far = product(second_query, second_key.T)

    def mixture_only(score_part, first_part, second_part):
        return head_mixture(score_part, first_part, second_part, band_ok, causal, position)

    mixture, mixture_pull = jax.vjp(mixture_only, scores, near_far, tanh_far)
    mixture_b = mixture.astype(jnp.bfloat16)
    head_out = product(mixture_b, head_value).astype(jnp.bfloat16)
    grad_mixture = product(grad_head, head_value.T)
    grad_value = product(mixture_b.T, grad_head)
    grad_scores, grad_first, grad_second = [
        piece.astype(jnp.bfloat16) for piece in mixture_pull(grad_mixture)
    ]
    grad_query = product(grad_scores, head_key)
    grad_key = product(grad_scores.T, head_query)
    pulled = feature_pull(
        (
            product(grad_first, first_key),
            product(grad_first.T, first_query),
            product(grad_second, second_key),
            product(grad_second.T, second_query),
        )
    )
    return (head_out, grad_query + pulled[0], grad_key + pulled[1], grad_value)


def head_split(values):
    item_count, length = (values.shape[0], values.shape[1])
    return (
        values.reshape(item_count, length, HEADS, HD)
        .transpose(0, 2, 1, 3)
        .reshape(item_count * HEADS, length, HD)
    )


def join_heads(per_head, item_count):
    length = per_head.shape[1]
    return (
        per_head.reshape(item_count, HEADS, length, HD)
        .transpose(0, 2, 1, 3)
        .reshape(item_count, length, HEADS * HD)
    )


def split_packed(packed):
    item_count, length = (packed.shape[0], packed.shape[1])
    split_parts = (
        packed.reshape(item_count, length, 3, HEADS, HD)
        .transpose(2, 0, 3, 1, 4)
        .reshape(3, item_count * HEADS, length, HD)
    )
    return (split_parts[0], split_parts[1], split_parts[2])


def attend_forward(stream, weight_set):
    mixer, output, gain = weight_set
    normed = norm_scale(stream, gain.astype(jnp.float32)).astype(jnp.bfloat16)
    packed = jnp.einsum("ild,de->ile", normed, mixer, preferred_element_type=jnp.float32).astype(
        jnp.bfloat16
    )
    per_head = lax.map(head_forward, split_packed(packed))
    joined = join_heads(per_head, stream.shape[0])
    return stream + jnp.einsum("ild,de->ile", joined, output, preferred_element_type=jnp.float32)


def attend_backward(stream, grad_in, weight_set):
    mixer, output, gain = weight_set
    item_count, length = (stream.shape[0], stream.shape[1])
    normed, norm_pull = jax.vjp(norm_scale, stream, gain.astype(jnp.float32))
    normed_b = normed.astype(jnp.bfloat16)
    packed = jnp.einsum("ild,de->ile", normed_b, mixer, preferred_element_type=jnp.float32).astype(
        jnp.bfloat16
    )
    head_query, head_key, head_value = split_packed(packed)
    grad_b = grad_in.astype(jnp.bfloat16)
    grad_joined = jnp.einsum(
        "ile,de->ild", grad_b, output, preferred_element_type=jnp.float32
    ).astype(jnp.bfloat16)
    head_out, grad_query, grad_key, grad_value = lax.map(
        head_backward, (head_query, head_key, head_value, head_split(grad_joined))
    )
    joined = join_heads(head_out, item_count)
    grad_output = jnp.einsum("ild,ile->de", joined, grad_b, preferred_element_type=jnp.float32)
    stacked = jnp.stack([grad_query, grad_key, grad_value])
    grad_packed = (
        stacked.reshape(3, item_count, HEADS, length, HD)
        .transpose(1, 3, 0, 2, 4)
        .reshape(item_count, length, 3 * HEADS * HD)
        .astype(jnp.bfloat16)
    )
    grad_mixer = jnp.einsum(
        "ild,ile->de", normed_b, grad_packed, preferred_element_type=jnp.float32
    )
    grad_normed = jnp.einsum("ile,de->ild", grad_packed, mixer, preferred_element_type=jnp.float32)
    grad_stream, grad_gain = norm_pull(grad_normed)
    return (grad_in + grad_stream, (grad_mixer, grad_output, grad_gain))


def feed_apply(stream, weight_set):
    expand, reduce_matrix, gain = (weight_set[0], weight_set[1], weight_set[2])
    normed = norm_scale(stream, gain.astype(jnp.float32)).astype(jnp.bfloat16)
    hidden = jnp.einsum("ild,df->ilf", normed, expand, preferred_element_type=jnp.float32)
    active = jax.nn.gelu(hidden).astype(jnp.bfloat16)
    return stream + jnp.einsum(
        "ilf,fd->ild", active, reduce_matrix, preferred_element_type=jnp.float32
    )


def feed_backward(stream, grad_in, weight_set):
    expand, reduce_matrix, gain = (weight_set[0], weight_set[1], weight_set[2])
    normed, norm_pull = jax.vjp(norm_scale, stream, gain.astype(jnp.float32))
    normed_b = normed.astype(jnp.bfloat16)
    hidden = jnp.einsum("ild,df->ilf", normed_b, expand, preferred_element_type=jnp.float32)
    active, gelu_pull = jax.vjp(jax.nn.gelu, hidden)
    active_b = active.astype(jnp.bfloat16)
    grad_b = grad_in.astype(jnp.bfloat16)
    grad_reduce = jnp.einsum("ilf,ild->fd", active_b, grad_b, preferred_element_type=jnp.float32)
    grad_active = jnp.einsum(
        "ild,fd->ilf", grad_b, reduce_matrix, preferred_element_type=jnp.float32
    )
    grad_hidden = gelu_pull(grad_active)[0].astype(jnp.bfloat16)
    grad_expand = jnp.einsum(
        "ild,ilf->df", normed_b, grad_hidden, preferred_element_type=jnp.float32
    )
    grad_normed = jnp.einsum("ilf,df->ild", grad_hidden, expand, preferred_element_type=jnp.float32)
    grad_stream, grad_gain = norm_pull(grad_normed)
    return (grad_in + grad_stream, (grad_expand, grad_reduce, grad_gain))


def body(
    tokens,
    padding_mask,
    embedding,
    mixer_weight,
    output_weight,
    mixer_gain,
    expand_weight,
    reduce_weight,
    feed_gain,
    final_gain,
):
    segments = lax.axis_size("section")
    segment_index = lax.axis_index("section")
    layer_index = segment_index // 2
    is_attention = segment_index % 2 == 0
    is_last = segment_index == segments - 1
    item_count = tokens.shape[0] // MICRO
    length = tokens.shape[1]
    slice_width = embedding.shape[1]
    row_part = embedding.shape[0]
    unit_part = reduce_weight.shape[1]
    token_ids = tokens.reshape(MICRO, item_count, length)
    pad_rows = padding_mask.reshape(MICRO, item_count, length)
    table_b = embedding.astype(jnp.bfloat16)

    def select_layer(stacked):
        return lax.dynamic_index_in_dim(stacked, layer_index, 0, keepdims=False).astype(
            jnp.bfloat16
        )

    attention_block = jnp.concatenate(
        [
            select_layer(mixer_weight),
            select_layer(output_weight),
            jnp.zeros((row_part, 2 * FF - 4 * D), jnp.bfloat16),
        ],
        axis=1,
    )
    feed_block = jnp.concatenate(
        [select_layer(expand_weight), select_layer(reduce_weight).reshape(row_part, FF)], axis=1
    )
    local_block = jnp.where(is_attention, attention_block, feed_block)
    local_gain = jnp.where(is_attention, select_layer(mixer_gain), select_layer(feed_gain))
    local_small = jnp.concatenate(
        [local_gain[:, None], final_gain.astype(jnp.bfloat16)[:, None], table_b], axis=1
    )
    whole_block, whole_small = (
        lax.all_gather(local_block, "dp", axis=0, tiled=True),
        lax.all_gather(local_small, "dp", axis=0, tiled=True),
    )
    attention_set = (whole_block[:, : 3 * D], whole_block[:, 3 * D : 4 * D], whole_small[:, 0])
    feed_set = (
        whole_block[:, :FF],
        whole_block[:, FF:].reshape(FF, D),
        whole_small[:, 0],
        whole_small[:, 1],
    )
    table_slice = whole_small[:, 2:]
    vocab_ids = (
        lax.broadcasted_iota(jnp.int32, (1, 1, 1, slice_width), 3) + segment_index * slice_width
    )
    slice_hot = token_ids[..., None] == vocab_ids
    full_ids = lax.broadcasted_iota(jnp.int32, (1, 1, 1, VOCAB), 3)
    partial_value = jnp.einsum(
        "mils,ds->mild",
        slice_hot.astype(jnp.bfloat16),
        table_slice,
        preferred_element_type=jnp.float32,
    ).astype(jnp.bfloat16)
    embedded = lax.psum(partial_value, "section").astype(jnp.float32)

    def attention_step(values):
        return attend_forward(values, attention_set)

    def feed_step(values):
        return feed_apply(values, feed_set)

    def forward_either(values):
        return lax.cond(is_attention, attention_step, feed_step, values)

    def unchanged(values):
        return values

    def forward_tick(moment, carried):
        received, saved, finals = carried
        micro_index = moment - segment_index
        active = (micro_index >= 0) & (micro_index < MICRO)
        slot_index = jnp.clip(micro_index, 0, MICRO - 1)
        stream_in = jnp.where(segment_index == 0, embedded[slot_index], received)
        saved = saved.at[slot_index].set(jnp.where(active, stream_in, saved[slot_index]))
        stream_out = lax.cond(active, forward_either, unchanged, stream_in)
        finals = finals.at[slot_index].set(
            jnp.where(active & is_last, stream_out, finals[slot_index])
        )
        received = shifted_2(stream_out, "section", 1)
        return (received, saved, finals)

    empty_stack = jnp.zeros((MICRO, item_count, length, D), jnp.float32)
    zero_rows = jnp.zeros((item_count, length, D), jnp.float32)
    received, saved, finals = lax.fori_loop(
        0, MICRO + segments - 1, forward_tick, (zero_rows, empty_stack, empty_stack)
    )
    normed_final, final_pull = jax.vjp(norm_scale, finals, feed_set[3].astype(jnp.float32))
    normed_b = normed_final.astype(jnp.bfloat16)
    zero_col = jnp.zeros((MICRO, item_count, 1), jnp.int32)
    targets = jnp.concatenate([token_ids[..., 1:], zero_col], axis=-1)
    scored = jnp.concatenate([pad_rows[..., 1:], zero_col], axis=-1).astype(jnp.float32)
    whole_table = lax.all_gather(table_slice, "section", axis=1, tiled=True)

    def head_here(operand):
        logits = jnp.einsum(
            "mild,dn->miln", normed_b, whole_table, preferred_element_type=jnp.float32
        )
        target_hot = (targets[..., None] == full_ids).astype(jnp.float32)
        peak = jnp.max(logits, axis=-1)
        spread_log = peak + jnp.log(jnp.sum(jnp.exp(logits - peak[..., None]), axis=-1))
        picked = jnp.sum(logits * target_hot, axis=-1)
        cross_terms = (spread_log - picked) * scored
        losses = (jnp.sum(cross_terms, axis=-1) / jnp.sum(scored, axis=-1)).reshape(-1)
        grads_full = (jnp.exp(logits - spread_log[..., None]) - target_hot) * scored[..., None]
        grads_b = grads_full.astype(jnp.bfloat16)
        table_full = jnp.einsum(
            "mild,miln->dn", normed_b, grads_b, preferred_element_type=jnp.float32
        )
        hidden = jnp.einsum(
            "miln,dn->mild", grads_b, whole_table, preferred_element_type=jnp.float32
        )
        return (losses, grads_full, table_full, hidden)

    def head_absent(operand):
        return (
            jnp.zeros((MICRO * item_count,), jnp.float32),
            jnp.zeros((MICRO, item_count, length, VOCAB), jnp.float32),
            jnp.zeros((D, VOCAB), jnp.float32),
            jnp.zeros((MICRO, item_count, length, D), jnp.float32),
        )

    losses, grads_full, table_full, hidden_grad = lax.cond(is_last, head_here, head_absent, 0)
    loss_copies = jnp.broadcast_to(losses[:, None], (losses.shape[0], segments))
    shares = (
        lax.psum_scatter(
            grads_full.astype(jnp.bfloat16), "section", scatter_dimension=3, tiled=True
        ).astype(jnp.float32),
        lax.psum_scatter(
            table_full.astype(jnp.bfloat16), "section", scatter_dimension=1, tiled=True
        ).astype(jnp.float32),
        lax.psum_scatter(
            loss_copies.astype(jnp.bfloat16), "section", scatter_dimension=1, tiled=True
        ).astype(jnp.float32),
    )
    logit_grad = shares[0]
    table_head = shares[1]
    item_loss = shares[2][:, 0]
    final_grad, final_gain_term = final_pull(hidden_grad)
    final_gain_term = jnp.where(is_last, final_gain_term, 0.0)
    zero_grads = (
        jnp.zeros((D, 3 * D), jnp.float32),
        jnp.zeros((D, D), jnp.float32),
        jnp.zeros((D,), jnp.float32),
        jnp.zeros((D, FF), jnp.float32),
        jnp.zeros((FF, D), jnp.float32),
        jnp.zeros((D,), jnp.float32),
    )

    def attention_back(operands):
        grad_stream, terms = attend_backward(operands[0], operands[1], attention_set)
        return (
            grad_stream,
            (terms[0], terms[1], terms[2], zero_grads[3], zero_grads[4], zero_grads[5]),
        )

    def feed_back(operands):
        grad_stream, terms = feed_backward(operands[0], operands[1], feed_set)
        return (
            grad_stream,
            (zero_grads[0], zero_grads[1], zero_grads[2], terms[0], terms[1], terms[2]),
        )

    def backward_either(operands):
        return lax.cond(is_attention, attention_back, feed_back, operands)

    def backward_skip(operands):
        return (jnp.zeros_like(operands[1]), zero_grads)

    def backward_tick(moment, carried):
        received, grad_sums, input_grads = carried
        step_count = moment - (segments - 1 - segment_index)
        active = (step_count >= 0) & (step_count < MICRO)
        slot_index = jnp.clip(MICRO - 1 - step_count, 0, MICRO - 1)
        grad_in = jnp.where(is_last, final_grad[slot_index], received)
        grad_out, increments = lax.cond(
            active, backward_either, backward_skip, (saved[slot_index], grad_in)
        )
        grad_sums = jax.tree.map(jnp.add, grad_sums, increments)
        input_grads = input_grads.at[slot_index].set(
            jnp.where(active & (segment_index == 0), grad_out, input_grads[slot_index])
        )
        received = shifted_2(grad_out.astype(jnp.bfloat16), "section", -1).astype(grad_out.dtype)
        return (received, grad_sums, input_grads)

    received, grad_sums, input_grads = lax.fori_loop(
        0, MICRO + segments - 1, backward_tick, (zero_rows, zero_grads, empty_stack)
    )
    spread_grads = spread(input_grads.astype(jnp.bfloat16), "section", 0).astype(input_grads.dtype)
    table_lookup = jnp.einsum(
        "mild,mils->ds",
        spread_grads,
        slice_hot.astype(jnp.float32),
        precision=lax.Precision.HIGHEST,
    )
    table_term = table_head + table_lookup
    attention_grad_block = jnp.concatenate(
        [grad_sums[0], grad_sums[1], jnp.zeros((D, 2 * FF - 4 * D), jnp.float32)], axis=1
    )
    feed_grad_block = jnp.concatenate([grad_sums[3], grad_sums[4].reshape(D, FF)], axis=1)
    grad_block = jnp.where(is_attention, attention_grad_block, feed_grad_block)
    gain_term = jnp.where(is_attention, grad_sums[2], grad_sums[5])
    grad_small = jnp.concatenate([gain_term[:, None], final_gain_term[:, None], table_term], axis=1)
    block_shard, small_shard = (
        lax.psum_scatter(grad_block, "dp", scatter_dimension=0, tiled=True),
        lax.psum_scatter(grad_small, "dp", scatter_dimension=0, tiled=True),
    )
    table_grad = small_shard[:, 2:]

    def to_slot(shard, keep):
        slots = jnp.zeros((2,) + shard.shape, jnp.float32)
        return lax.dynamic_update_index_in_dim(slots, jnp.where(keep, shard, 0.0), layer_index, 0)

    is_feed = jnp.logical_not(is_attention)
    summed = (
        lax.psum(
            to_slot(block_shard[:, : 3 * D], is_attention).astype(jnp.bfloat16), "section"
        ).astype(jnp.float32),
        lax.psum(
            to_slot(block_shard[:, 3 * D : 4 * D], is_attention).astype(jnp.bfloat16), "section"
        ).astype(jnp.float32),
        lax.psum(to_slot(small_shard[:, 0], is_attention).astype(jnp.bfloat16), "section").astype(
            jnp.float32
        ),
        lax.psum(to_slot(block_shard[:, :FF], is_feed).astype(jnp.bfloat16), "section").astype(
            jnp.float32
        ),
        lax.psum(
            to_slot(block_shard[:, FF:].reshape(unit_part, D), is_feed).astype(jnp.bfloat16),
            "section",
        ).astype(jnp.float32),
        lax.psum(to_slot(small_shard[:, 0], is_feed).astype(jnp.bfloat16), "section").astype(
            jnp.float32
        ),
        lax.psum(small_shard[:, 1].astype(jnp.bfloat16), "section").astype(jnp.float32),
    )
    return (
        item_loss,
        logit_grad.reshape(MICRO * item_count, length, slice_width),
        table_grad,
        summed[0],
        summed[1],
        summed[2],
        summed[3],
        summed[4],
        summed[5],
        summed[6],
    )


def solution(mesh):
    placed = (
        P("dp", None),
        P("dp", None),
        P("dp", "section"),
        P(None, "dp", None),
        P(None, "dp", None),
        P(None, "dp"),
        P(None, "dp", None),
        P(None, "dp", None),
        P(None, "dp"),
        P("dp"),
    )
    return jax.shard_map(
        body,
        mesh=mesh,
        in_specs=placed,
        out_specs=(
            P("dp"),
            P("dp", None, "section"),
            P("dp", "section"),
            P(None, "dp", None),
            P(None, "dp", None),
            P(None, "dp"),
            P(None, "dp", None),
            P(None, "dp", None),
            P(None, "dp"),
            P("dp"),
        ),
        check_vma=False,
    )
```

profile of v0, /device:TPU:0, one launch (start us, length us, event | category | flops | bytes accessed | tf_op | source)
XLA Modules:
  0.0 1949.1 jit_solution(3966150709614247779)
XLA Ops:
  10.6 10.7 all_gather.9
  30.3 17.4 all_gather.11
  51.0 82.7 %all-reduce.8.cloned.1.call-done = bf16[4,1,640,512]{3,2,0,1:T(8,128)(2,1)} async-done(((bf16[4,1,640,512]{3,2,0,1:T(8,128)(2,1)}), bf16[4,1,640,512]{3,2,0,1:T(8,128)(2,1)}) %all-reduce.8.cloned.1.call-update) | async-done | bytes 2621456 | tf_op jit(solution)/shard_map/psum | solution.py:288
  133.6 4.8 bitcast_convert_fusion.1
  155.7 575.6 %while.79 = (s32[]{:T(128)}, f32[1,640,512]{2,1,0:T(8,128)S(1)}, f32[4,1,640,512]{3,2,1,0:T(8,128)}, f32[4,1,640,512]{3,2,1,0:T(8,128)}, s32[]{:T(128)}, /*index...) while((s32[]{:T(128)}, f32[1,640,512]{2,1,0:T(8,128)S(1)}, ...), condition=%wide.region_14.15_spmd, body=%wide.region_1.14_spmd.sunk | while | flops 2699756544 | bytes 48347716 | solution.py:318
  161.5 64.7 %conditional.9 = (f32[1,640,512]{2,1,0:T(8,128)S(1)}) conditional(s32[]{:T(128)} %convert_element_type.818, f32[1,640,512]{2,1,0:T(8,128)S(1)} %get-tuple-element.1834, (pred[]{:T(512)}, f32[1,640,512]{2,1,0:T(8,128)S(1)}, bf16[512]{0:T(512)(128)(2,1)S(1)}, bf16[512,2048]{1,0:T(8,128)(2,1)}, bf16[2048,512]{1,0:T(8,128)(2,1)}, ...), branch_computations={%region_2.2_spmd, %region_3.12_spmd} | conditional | flops 2698118144 | bytes 27373260 | solution.py:309
  161.5 64.7 %conditional = (f32[1,640,512]{2,1,0:T(8,128)S(1)}) conditional(s32[]{:T(128)} %convert_element_type.300, (f32[1,640,512]{2,1,0:T(8,128)S(1)}, bf16[512]{0:T(512)(128)(2,1)S(1)}, bf16[512,2048]{1,0:T(8,128)(2,1)}, bf16[2048,512]{1,0:T(8,128)(2,1)}) %tuple.111, (f32[1,640,512]{2,1,0:T(8,128)S(1)}, bf16[512]{0:T(512)(128)(2,1)S(1)}, ...), branch_computations={%region_4.4_spmd, %region_6.11_spmd} | conditional | flops 2698118144 | bytes 27373192 | solution.py:297
  172.5 51.9 %while.77 = (s32[]{:T(128)}, bf16[8,640,64]{1,2,0:T(8,128)(2,1)}, bf16[8,640,64]{1,2,0:T(8,128)(2,1)}, bf16[8,640,64]{1,2,0:T(8,128)(2,1)}, bf16[8,640,64]{1,2,0:T(8,128)(2,1)}, /*index=5*/s32[]{:T(128)}) while((s32[]{:T(128)}, bf16[8,640,64]{1,2,0:T(8,128)(2,1)}, bf16[8,640,64]{1,2,0:T(8,128)(2,1)}, bf16[8,640,64]{1,2,0:T(8,128)(2,1)}, ...), condition=%wide.region_12.10_spmd, body=%wide.region_8.9_spmd.sunk | while | flops 222699520 | bytes 9531977 | solution.py:149
  231.1 24.7 %collective-permute-done.1 = f32[1,640,512]{2,1,0:T(8,128)S(1)} collective-permute-done((f32[1,640,512]{2,1,0:T(8,128)S(1)}, f32[1,640,512]{2,1,0:T(8,128)S(1)}, u32[]{:S(2)}, u32[]{:S(2)}) %collective-permute-start.1) | collective-permute-done | bytes 1310752 | tf_op jit(solution)/shard_map/while/body/eval_jaxpr/ppermute | solution.py:18
  261.5 64.7 %conditional.9 = (f32[1,640,512]{2,1,0:T(8,128)S(1)}) conditional(s32[]{:T(128)} %convert_element_type.818, f32[1,640,512]{2,1,0:T(8,128)S(1)} %get-tuple-element.1834, (pred[]{:T(512)}, f32[1,640,512]{2,1,0:T(8,128)S(1)}, bf16[512]{0:T(512)(128)(2,1)S(1)}, bf16[512,2048]{1,0:T(8,128)(2,1)}, bf16[2048,512]{1,0:T(8,128)(2,1)}, ...), branch_computations={%region_2.2_spmd, %region_3.12_spmd} | conditional | flops 2698118144 | bytes 27373260 | solution.py:309
  261.5 64.7 %conditional = (f32[1,640,512]{2,1,0:T(8,128)S(1)}) conditional(s32[]{:T(128)} %convert_element_type.300, (f32[1,640,512]{2,1,0:T(8,128)S(1)}, bf16[512]{0:T(512)(128)(2,1)S(1)}, bf16[512,2048]{1,0:T(8,128)(2,1)}, bf16[2048,512]{1,0:T(8,128)(2,1)}) %tuple.111, (f32[1,640,512]{2,1,0:T(8,128)S(1)}, bf16[512]{0:T(512)(128)(2,1)S(1)}, ...), branch_computations={%region_4.4_spmd, %region_6.11_spmd} | conditional | flops 2698118144 | bytes 27373192 | solution.py:297
  261.7 4.0 convolution_convert_fusion
  272.5 51.9 %while.77 = (s32[]{:T(128)}, bf16[8,640,64]{1,2,0:T(8,128)(2,1)}, bf16[8,640,64]{1,2,0:T(8,128)(2,1)}, bf16[8,640,64]{1,2,0:T(8,128)(2,1)}, bf16[8,640,64]{1,2,0:T(8,128)(2,1)}, /*index=5*/s32[]{:T(128)}) while((s32[]{:T(128)}, bf16[8,640,64]{1,2,0:T(8,128)(2,1)}, bf16[8,640,64]{1,2,0:T(8,128)(2,1)}, bf16[8,640,64]{1,2,0:T(8,128)(2,1)}, ...), condition=%wide.region_12.10_spmd, body=%wide.region_8.9_spmd.sunk | while | flops 222699520 | bytes 9531977 | solution.py:149
  331.1 24.1 %collective-permute-done.1 = f32[1,640,512]{2,1,0:T(8,128)S(1)} collective-permute-done((f32[1,640,512]{2,1,0:T(8,128)S(1)}, f32[1,640,512]{2,1,0:T(8,128)S(1)}, u32[]{:S(2)}, u32[]{:S(2)}) %collective-permute-start.1) | collective-permute-done | bytes 1310752 | tf_op jit(solution)/shard_map/while/body/eval_jaxpr/ppermute | solution.py:18
  361.1 64.7 %conditional.9 = (f32[1,640,512]{2,1,0:T(8,128)S(1)}) conditional(s32[]{:T(128)} %convert_element_type.818, f32[1,640,512]{2,1,0:T(8,128)S(1)} %get-tuple-element.1834, (pred[]{:T(512)}, f32[1,640,512]{2,1,0:T(8,128)S(1)}, bf16[512]{0:T(512)(128)(2,1)S(1)}, bf16[512,2048]{1,0:T(8,128)(2,1)}, bf16[2048,512]{1,0:T(8,128)(2,1)}, ...), branch_computations={%region_2.2_spmd, %region_3.12_spmd} | conditional | flops 2698118144 | bytes 27373260 | solution.py:309
  361.1 64.7 %conditional = (f32[1,640,512]{2,1,0:T(8,128)S(1)}) conditional(s32[]{:T(128)} %convert_element_type.300, (f32[1,640,512]{2,1,0:T(8,128)S(1)}, bf16[512]{0:T(512)(128)(2,1)S(1)}, bf16[512,2048]{1,0:T(8,128)(2,1)}, bf16[2048,512]{1,0:T(8,128)(2,1)}) %tuple.111, (f32[1,640,512]{2,1,0:T(8,128)S(1)}, bf16[512]{0:T(512)(128)(2,1)S(1)}, ...), branch_computations={%region_4.4_spmd, %region_6.11_spmd} | conditional | flops 2698118144 | bytes 27373192 | solution.py:297
  361.3 4.0 convolution_convert_fusion
  372.1 51.9 %while.77 = (s32[]{:T(128)}, bf16[8,640,64]{1,2,0:T(8,128)(2,1)}, bf16[8,640,64]{1,2,0:T(8,128)(2,1)}, bf16[8,640,64]{1,2,0:T(8,128)(2,1)}, bf16[8,640,64]{1,2,0:T(8,128)(2,1)}, /*index=5*/s32[]{:T(128)}) while((s32[]{:T(128)}, bf16[8,640,64]{1,2,0:T(8,128)(2,1)}, bf16[8,640,64]{1,2,0:T(8,128)(2,1)}, bf16[8,640,64]{1,2,0:T(8,128)(2,1)}, ...), condition=%wide.region_12.10_spmd, body=%wide.region_8.9_spmd.sunk | while | flops 222699520 | bytes 9531977 | solution.py:149
  430.7 23.5 %collective-permute-done.1 = f32[1,640,512]{2,1,0:T(8,128)S(1)} collective-permute-done((f32[1,640,512]{2,1,0:T(8,128)S(1)}, f32[1,640,512]{2,1,0:T(8,128)S(1)}, u32[]{:S(2)}, u32[]{:S(2)}) %collective-permute-start.1) | collective-permute-done | bytes 1310752 | tf_op jit(solution)/shard_map/while/body/eval_jaxpr/ppermute | solution.py:18
  459.9 64.7 %conditional.9 = (f32[1,640,512]{2,1,0:T(8,128)S(1)}) conditional(s32[]{:T(128)} %convert_element_type.818, f32[1,640,512]{2,1,0:T(8,128)S(1)} %get-tuple-element.1834, (pred[]{:T(512)}, f32[1,640,512]{2,1,0:T(8,128)S(1)}, bf16[512]{0:T(512)(128)(2,1)S(1)}, bf16[512,2048]{1,0:T(8,128)(2,1)}, bf16[2048,512]{1,0:T(8,128)(2,1)}, ...), branch_computations={%region_2.2_spmd, %region_3.12_spmd} | conditional | flops 2698118144 | bytes 27373260 | solution.py:309
  459.9 64.7 %conditional = (f32[1,640,512]{2,1,0:T(8,128)S(1)}) conditional(s32[]{:T(128)} %convert_element_type.300, (f32[1,640,512]{2,1,0:T(8,128)S(1)}, bf16[512]{0:T(512)(128)(2,1)S(1)}, bf16[512,2048]{1,0:T(8,128)(2,1)}, bf16[2048,512]{1,0:T(8,128)(2,1)}) %tuple.111, (f32[1,640,512]{2,1,0:T(8,128)S(1)}, bf16[512]{0:T(512)(128)(2,1)S(1)}, ...), branch_computations={%region_4.4_spmd, %region_6.11_spmd} | conditional | flops 2698118144 | bytes 27373192 | solution.py:297
  460.1 4.0 convolution_convert_fusion
  470.9 51.9 %while.77 = (s32[]{:T(128)}, bf16[8,640,64]{1,2,0:T(8,128)(2,1)}, bf16[8,640,64]{1,2,0:T(8,128)(2,1)}, bf16[8,640,64]{1,2,0:T(8,128)(2,1)}, bf16[8,640,64]{1,2,0:T(8,128)(2,1)}, /*index=5*/s32[]{:T(128)}) while((s32[]{:T(128)}, bf16[8,640,64]{1,2,0:T(8,128)(2,1)}, bf16[8,640,64]{1,2,0:T(8,128)(2,1)}, bf16[8,640,64]{1,2,0:T(8,128)(2,1)}, ...), condition=%wide.region_12.10_spmd, body=%wide.region_8.9_spmd.sunk | while | flops 222699520 | bytes 9531977 | solution.py:149
  529.5 22.8 %collective-permute-done.1 = f32[1,640,512]{2,1,0:T(8,128)S(1)} collective-permute-done((f32[1,640,512]{2,1,0:T(8,128)S(1)}, f32[1,640,512]{2,1,0:T(8,128)S(1)}, u32[]{:S(2)}, u32[]{:S(2)}) %collective-permute-start.1) | collective-permute-done | bytes 1310752 | tf_op jit(solution)/shard_map/while/body/eval_jaxpr/ppermute | solution.py:18
  558.1 10.1 collective-permute-start.1
  571.7 21.9 %collective-permute-done.1 = f32[1,640,512]{2,1,0:T(8,128)S(1)} collective-permute-done((f32[1,640,512]{2,1,0:T(8,128)S(1)}, f32[1,640,512]{2,1,0:T(8,128)S(1)}, u32[]{:S(2)}, u32[]{:S(2)}) %collective-permute-start.1) | collective-permute-done | bytes 1310752 | tf_op jit(solution)/shard_map/while/body/eval_jaxpr/ppermute | solution.py:18
  599.4 9.9 collective-permute-start.1
  612.8 20.5 %collective-permute-done.1 = f32[1,640,512]{2,1,0:T(8,128)S(1)} collective-permute-done((f32[1,640,512]{2,1,0:T(8,128)S(1)}, f32[1,640,512]{2,1,0:T(8,128)S(1)}, u32[]{:S(2)}, u32[]{:S(2)}) %collective-permute-start.1) | collective-permute-done | bytes 1310752 | tf_op jit(solution)/shard_map/while/body/eval_jaxpr/ppermute | solution.py:18
  639.0 69.2 %collective-permute-start.1 = (f32[1,640,512]{2,1,0:T(8,128)S(1)}, f32[1,640,512]{2,1,0:T(8,128)S(1)}, u32[]{:S(2)}, u32[]{:S(2)}) collective-permute-start(f32[1,640,512]{2,1,0:T(8,128)S(1)} %get-tuple-element.2132), channel_id=1, source_target_pairs={{0,8},{8,16},{16,24},{1,9},{9,17},{17,25},{2,10},{10,18},{18,26},{... | collective-permute-start | bytes 3932168 | tf_op jit(solution)/shard_map/while/body/eval_jaxpr/ppermute | solution.py:18
  711.7 19.5 %collective-permute-done.1 = f32[1,640,512]{2,1,0:T(8,128)S(1)} collective-permute-done((f32[1,640,512]{2,1,0:T(8,128)S(1)}, f32[1,640,512]{2,1,0:T(8,128)S(1)}, u32[]{:S(2)}, u32[]{:S(2)}) %collective-permute-start.1) | collective-permute-done | bytes 1310752 | tf_op jit(solution)/shard_map/while/body/eval_jaxpr/ppermute | solution.py:18
  736.3 5.3 conditional.5
  741.6 5.8 fusion.269
  747.4 4.6 add_add_fusion.2
  752.1 870.2 %while.80 = (s32[]{:T(128)}, f32[1,640,512]{2,1,0:T(8,128)}, f32[512,1536]{1,0:T(8,128)}, f32[512,512]{1,0:T(8,128)}, f32[512]{0:T(512)}, /*index=5*/f32[512,204...) while((s32[]{:T(128)}, f32[1,640,512]{2,1,0:T(8,128)}, ...), condition=%wide.region_47.48_spmd.clone, body=%wide.region_26.47_spmd.clone.sunk | while | flops 6764369920 | bytes 224731568 | solution.py:419
  753.6 10.1 conditional.10
  767.0 5.5 select_add_fusion.14
  787.8 10.1 conditional.10
  801.2 6.7 select_add_fusion.14
  823.3 10.1 conditional.10
  836.7 6.7 select_add_fusion.14
  855.9 132.4 %collective-permute-done = bf16[1,640,512]{2,1,0:T(8,128)(2,1)} collective-permute-done((bf16[1,640,512]{2,1,0:T(8,128)(2,1)}, bf16[1,640,512]{2,1,0:T(8,128)(2,1)}, u32[]{:S(2)}, u32[]{:S(2)}) %collective-permute-start) | collective-permute-done | bytes 655392 | tf_op jit(solution)/shard_map/while/body/eval_jaxpr/ppermute | solution.py:18
  990.7 131.3 %conditional.10 = ((bf16[1,640,512]{2,1,0:T(8,128)(2,1)}, f32[512,1536]{1,0:T(8,128)}, f32[512,512]{1,0:T(8,128)}, f32[512]{0:T(512)}, f32[512,2048]{1,0:T(8,128)}, /*index=5*/f32[2048,512]{1,0:T(8,128)}, f32[512]{0:T(512)})) conditional(s32[]{:T(128)} %convert_element_type.819, () %tuple.241, (pred[]{:T(512)}, f32[4,1,640,512]{3,2,1,0:T(8,128)}, ...), branch_computations={%region_27.27_spmd, %region_28.45_spmd} | conditional | flops 6757093376 | bytes 109341184 | solution.py:409
  994.0 128.0 %conditional.2 = (bf16[1,640,512]{2,1,0:T(8,128)(2,1)}, f32[512,1536]{1,0:T(8,128)}, f32[512,512]{1,0:T(8,128)}, f32[512]{0:T(512)}, f32[512,2048]{1,0:T(8,128)}, /*index=5*/f32[2048,512]{1,0:T(8,128)}, f32[512]{0:T(512)}) conditional(s32[]{:T(128)} %convert_element_type.342, (f32[1,640,512]{2,1,0:T(8,128)S(1)}, bf16[2048,512]{1,0:T(8,128)(2,1)}, ...), branch_computations={%region_29.31_spmd, %region_33.44_spmd} | conditional | flops 6756438016 | bytes 97544568 | solution.py:398
  1007.1 98.5 %while.78 = (s32[]{:T(128)}, bf16[8,640,64]{1,2,0:T(8,128)(2,1)}, bf16[8,640,64]{1,2,0:T(8,128)(2,1)}, bf16[8,640,64]{1,2,0:T(8,128)(2,1)}, bf16[8,640,64]{1,2,0...) while((s32[]{:T(128)}, bf16[8,640,64]{1,2,0:T(8,128)(2,1)}, ...), condition=%wide.region_43.41_spmd, body=%wide.region_35.40_spmd.sunk | while | flops 664414720 | bytes 38778020 | solution.py:167
  1125.3 6.7 select_add_fusion.14
  1148.5 131.3 %conditional.10 = ((bf16[1,640,512]{2,1,0:T(8,128)(2,1)}, f32[512,1536]{1,0:T(8,128)}, f32[512,512]{1,0:T(8,128)}, f32[512]{0:T(512)}, f32[512,2048]{1,0:T(8,128)}, /*index=5*/f32[2048,512]{1,0:T(8,128)}, f32[512]{0:T(512)})) conditional(s32[]{:T(128)} %convert_element_type.819, () %tuple.241, (pred[]{:T(512)}, f32[4,1,640,512]{3,2,1,0:T(8,128)}, ...), branch_computations={%region_27.27_spmd, %region_28.45_spmd} | conditional | flops 6757093376 | bytes 109341184 | solution.py:409
  1151.8 128.0 %conditional.2 = (bf16[1,640,512]{2,1,0:T(8,128)(2,1)}, f32[512,1536]{1,0:T(8,128)}, f32[512,512]{1,0:T(8,128)}, f32[512]{0:T(512)}, f32[512,2048]{1,0:T(8,128)}, /*index=5*/f32[2048,512]{1,0:T(8,128)}, f32[512]{0:T(512)}) conditional(s32[]{:T(128)} %convert_element_type.342, (f32[1,640,512]{2,1,0:T(8,128)S(1)}, bf16[2048,512]{1,0:T(8,128)(2,1)}, ...), branch_computations={%region_29.31_spmd, %region_33.44_spmd} | conditional | flops 6756438016 | bytes 97544568 | solution.py:398
  1165.0 98.5 %while.78 = (s32[]{:T(128)}, bf16[8,640,64]{1,2,0:T(8,128)(2,1)}, bf16[8,640,64]{1,2,0:T(8,128)(2,1)}, bf16[8,640,64]{1,2,0:T(8,128)(2,1)}, bf16[8,640,64]{1,2,0...) while((s32[]{:T(128)}, bf16[8,640,64]{1,2,0:T(8,128)(2,1)}, ...), condition=%wide.region_43.41_spmd, body=%wide.region_35.40_spmd.sunk | while | flops 664414720 | bytes 38778020 | solution.py:167
  1283.1 6.7 select_add_fusion.14
  1306.4 131.3 %conditional.10 = ((bf16[1,640,512]{2,1,0:T(8,128)(2,1)}, f32[512,1536]{1,0:T(8,128)}, f32[512,512]{1,0:T(8,128)}, f32[512]{0:T(512)}, f32[512,2048]{1,0:T(8,128)}, /*index=5*/f32[2048,512]{1,0:T(8,128)}, f32[512]{0:T(512)})) conditional(s32[]{:T(128)} %convert_element_type.819, () %tuple.241, (pred[]{:T(512)}, f32[4,1,640,512]{3,2,1,0:T(8,128)}, ...), branch_computations={%region_27.27_spmd, %region_28.45_spmd} | conditional | flops 6757093376 | bytes 109341184 | solution.py:409
  1309.7 128.0 %conditional.2 = (bf16[1,640,512]{2,1,0:T(8,128)(2,1)}, f32[512,1536]{1,0:T(8,128)}, f32[512,512]{1,0:T(8,128)}, f32[512]{0:T(512)}, f32[512,2048]{1,0:T(8,128)}, /*index=5*/f32[2048,512]{1,0:T(8,128)}, f32[512]{0:T(512)}) conditional(s32[]{:T(128)} %convert_element_type.342, (f32[1,640,512]{2,1,0:T(8,128)S(1)}, bf16[2048,512]{1,0:T(8,128)(2,1)}, ...), branch_computations={%region_29.31_spmd, %region_33.44_spmd} | conditional | flops 6756438016 | bytes 97544568 | solution.py:398
  1322.9 98.5 %while.78 = (s32[]{:T(128)}, bf16[8,640,64]{1,2,0:T(8,128)(2,1)}, bf16[8,640,64]{1,2,0:T(8,128)(2,1)}, bf16[8,640,64]{1,2,0:T(8,128)(2,1)}, bf16[8,640,64]{1,2,0...) while((s32[]{:T(128)}, bf16[8,640,64]{1,2,0:T(8,128)(2,1)}, ...), condition=%wide.region_43.41_spmd, body=%wide.region_35.40_spmd.sunk | while | flops 664414720 | bytes 38778020 | solution.py:167
  1441.0 6.7 select_add_fusion.14
  1464.2 131.3 %conditional.10 = ((bf16[1,640,512]{2,1,0:T(8,128)(2,1)}, f32[512,1536]{1,0:T(8,128)}, f32[512,512]{1,0:T(8,128)}, f32[512]{0:T(512)}, f32[512,2048]{1,0:T(8,128)}, /*index=5*/f32[2048,512]{1,0:T(8,128)}, f32[512]{0:T(512)})) conditional(s32[]{:T(128)} %convert_element_type.819, () %tuple.241, (pred[]{:T(512)}, f32[4,1,640,512]{3,2,1,0:T(8,128)}, ...), branch_computations={%region_27.27_spmd, %region_28.45_spmd} | conditional | flops 6757093376 | bytes 109341184 | solution.py:409
  1467.6 128.0 %conditional.2 = (bf16[1,640,512]{2,1,0:T(8,128)(2,1)}, f32[512,1536]{1,0:T(8,128)}, f32[512,512]{1,0:T(8,128)}, f32[512]{0:T(512)}, f32[512,2048]{1,0:T(8,128)}, /*index=5*/f32[2048,512]{1,0:T(8,128)}, f32[512]{0:T(512)}) conditional(s32[]{:T(128)} %convert_element_type.342, (f32[1,640,512]{2,1,0:T(8,128)S(1)}, bf16[2048,512]{1,0:T(8,128)(2,1)}, ...), branch_computations={%region_29.31_spmd, %region_33.44_spmd} | conditional | flops 6756438016 | bytes 97544568 | solution.py:398
  1480.7 98.5 %while.78 = (s32[]{:T(128)}, bf16[8,640,64]{1,2,0:T(8,128)(2,1)}, bf16[8,640,64]{1,2,0:T(8,128)(2,1)}, bf16[8,640,64]{1,2,0:T(8,128)(2,1)}, bf16[8,640,64]{1,2,0...) while((s32[]{:T(128)}, bf16[8,640,64]{1,2,0:T(8,128)(2,1)}, ...), condition=%wide.region_43.41_spmd, body=%wide.region_35.40_spmd.sunk | while | flops 664414720 | bytes 38778020 | solution.py:167
  1598.8 6.7 select_add_fusion.14
  1622.3 5.8 reshape.737
  1628.1 6.5 maximum_select_fusion
  1638.1 67.0 %reduce-scatter.11.cloned.1.call-done = f32[64,4096]{1,0:T(8,128)} async-done(((f32[512,4096]{1,0:T(8,128)}), f32[64,4096]{1,0:T(8,128)}) %reduce-scatter.11.cloned.1.call-update) | async-done | bytes 1048592 | tf_op jit(solution)/shard_map/reduce_scatter | solution.py:438
  1709.1 81.0 %reduce-scatter.9.cloned.1.call-done = bf16[512,64]{0,1:T(8,128)(2,1)} async-done(((bf16[512,256]{0,1:T(8,128)(2,1)}), bf16[512,64]{0,1:T(8,128)(2,1)}) %reduce-scatter.9.cloned.1.call-update) | async-done | bytes 65552 | tf_op jit(solution)/shard_map/reduce_scatter | solution.py:362
  1790.1 98.0 %all-reduce.10.cloned.1.call-done = (bf16[4,640,512]{2,1,0:T(8,128)(2,1)}, bf16[2,64,1536]{2,1,0:T(8,128)(2,1)}, bf16[2,64,512]{2,1,0:T(8,128)(2,1)}, bf16[2,64,2048]{2,1,0:T(8,128)(2,1)}, bf16[2,256,512]{2,1,0:T(8,128)(2,1)}) async-done(((bf16[4,640,512]{2,1,0:T(8,128)(2,1)}, bf16[2,64,1536]{2,1,0:T(8,128)(2,1)}, bf16[2,64,512]{2,1,0:T(8,128)(2,1)}, bf16[2,64,2048]{2,1,0:T(8,128)(2,1)}, ...) | async-done | bytes 4194320 | tf_op jit(solution)/shard_map/psum | solution.py:23
  1897.2 27.0 %reduce-scatter.13.cloned.1.call-done = f32[64,66]{1,0:T(8,128)} async-done(((f32[512,66]{1,0:T(8,128)}), f32[64,66]{1,0:T(8,128)}) %reduce-scatter.13.cloned.1.call-update) | async-done | bytes 16912
  1925.3 11.7 all-reduce.3
  (1634 shorter events, 1065.5 us)
Async XLA Ops:
  8.0 17.0 copy-start
  8.0 125.6 %all-reduce.8.cloned.1.call-start = ((), (), s32[]{:S(2)}) async-start(), calls=%async_computation.4 | async-start | bytes 5242880 | tf_op jit(solution)/shard_map/psum | solution.py:288
  25.0 113.5 %all-gather.2.cloned.1.call-start = ((), (), s32[]{:S(2)}) async-start(), calls=%async_computation.5 | async-start | bytes 4718592 | tf_op jit(solution)/shard_map/all_gather | solution.py:266
  29.3 1675.8 %reduce-scatter.11.cloned.1.call-start = ((), (), s32[]{:S(2)}) async-start(), calls=%async_computation.8 | async-start | bytes 9437184 | tf_op jit(solution)/shard_map/reduce_scatter | solution.py:438
  226.2 29.6 %collective-permute-start.1 = (f32[1,640,512]{2,1,0:T(8,128)S(1)}, f32[1,640,512]{2,1,0:T(8,128)S(1)}, u32[]{:S(2)}, u32[]{:S(2)}) collective-permute-start(f32[1,640,512]{2,1,0:T(8,128)S(1)} %get-tuple-element.2132), channel_id=1, source_target_pairs={{0,8},{8,16},{16,24},{1,9},{9,17},{17,25},{2,10},{10,18},{18,26},{... | collective-permute-start | bytes 3932168 | tf_op jit(solution)/shard_map/while/body/eval_jaxpr/ppermute | solution.py:18
  326.3 29.0 %collective-permute-start.1 = (f32[1,640,512]{2,1,0:T(8,128)S(1)}, f32[1,640,512]{2,1,0:T(8,128)S(1)}, u32[]{:S(2)}, u32[]{:S(2)}) collective-permute-start(f32[1,640,512]{2,1,0:T(8,128)S(1)} %get-tuple-element.2132), channel_id=1, source_target_pairs={{0,8},{8,16},{16,24},{1,9},{9,17},{17,25},{2,10},{10,18},{18,26},{... | collective-permute-start | bytes 3932168 | tf_op jit(solution)/shard_map/while/body/eval_jaxpr/ppermute | solution.py:18
  425.8 28.3 %collective-permute-start.1 = (f32[1,640,512]{2,1,0:T(8,128)S(1)}, f32[1,640,512]{2,1,0:T(8,128)S(1)}, u32[]{:S(2)}, u32[]{:S(2)}) collective-permute-start(f32[1,640,512]{2,1,0:T(8,128)S(1)} %get-tuple-element.2132), channel_id=1, source_target_pairs={{0,8},{8,16},{16,24},{1,9},{9,17},{17,25},{2,10},{10,18},{18,26},{... | collective-permute-start | bytes 3932168 | tf_op jit(solution)/shard_map/while/body/eval_jaxpr/ppermute | solution.py:18
  524.7 27.7 %collective-permute-start.1 = (f32[1,640,512]{2,1,0:T(8,128)S(1)}, f32[1,640,512]{2,1,0:T(8,128)S(1)}, u32[]{:S(2)}, u32[]{:S(2)}) collective-permute-start(f32[1,640,512]{2,1,0:T(8,128)S(1)} %get-tuple-element.2132), channel_id=1, source_target_pairs={{0,8},{8,16},{16,24},{1,9},{9,17},{17,25},{2,10},{10,18},{18,26},{... | collective-permute-start | bytes 3932168 | tf_op jit(solution)/shard_map/while/body/eval_jaxpr/ppermute | solution.py:18
  558.1 35.5 %collective-permute-start.1 = (f32[1,640,512]{2,1,0:T(8,128)S(1)}, f32[1,640,512]{2,1,0:T(8,128)S(1)}, u32[]{:S(2)}, u32[]{:S(2)}) collective-permute-start(f32[1,640,512]{2,1,0:T(8,128)S(1)} %get-tuple-element.2132), channel_id=1, source_target_pairs={{0,8},{8,16},{16,24},{1,9},{9,17},{17,25},{2,10},{10,18},{18,26},{... | collective-permute-start | bytes 3932168 | tf_op jit(solution)/shard_map/while/body/eval_jaxpr/ppermute | solution.py:18
  599.4 33.9 %collective-permute-start.1 = (f32[1,640,512]{2,1,0:T(8,128)S(1)}, f32[1,640,512]{2,1,0:T(8,128)S(1)}, u32[]{:S(2)}, u32[]{:S(2)}) collective-permute-start(f32[1,640,512]{2,1,0:T(8,128)S(1)} %get-tuple-element.2132), channel_id=1, source_target_pairs={{0,8},{8,16},{16,24},{1,9},{9,17},{17,25},{2,10},{10,18},{18,26},{... | collective-permute-start | bytes 3932168 | tf_op jit(solution)/shard_map/while/body/eval_jaxpr/ppermute | solution.py:18
  639.0 92.2 %collective-permute-start.1 = (f32[1,640,512]{2,1,0:T(8,128)S(1)}, f32[1,640,512]{2,1,0:T(8,128)S(1)}, u32[]{:S(2)}, u32[]{:S(2)}) collective-permute-start(f32[1,640,512]{2,1,0:T(8,128)S(1)} %get-tuple-element.2132), channel_id=1, source_target_pairs={{0,8},{8,16},{16,24},{1,9},{9,17},{17,25},{2,10},{10,18},{18,26},{... | collective-permute-start | bytes 3932168 | tf_op jit(solution)/shard_map/while/body/eval_jaxpr/ppermute | solution.py:18
  731.3 4.0 copy-start.2
  731.3 4.0 copy-start.41
  741.6 5.8 copy-start.47
  741.6 5.9 slice-start
  741.6 5.9 slice-start.1
  763.7 21.3 %collective-permute-start = (bf16[1,640,512]{2,1,0:T(8,128)(2,1)}, bf16[1,640,512]{2,1,0:T(8,128)(2,1)}, u32[]{:S(2)}, u32[]{:S(2)}) collective-permute-start(bf16[1,640,512]{2,1,0:T(8,128)(2,1)} %get-tuple-element.1856), channel_id=1, source_target_pairs={{8,0},{16,8},{24,16},{9,1},{17,9},{25,17},{10,2},{18,10},{26,18},{... | collective-permute-start | bytes 1966088 | tf_op jit(solution)/shard_map/while/body/eval_jaxpr/ppermute | solution.py:18
  767.0 5.5 copy-start.3
  776.2 8.7 copy-start.4
  776.2 5.7 copy-start.5
  778.8 6.1 copy-start.14
  797.9 22.5 %collective-permute-start = (bf16[1,640,512]{2,1,0:T(8,128)(2,1)}, bf16[1,640,512]{2,1,0:T(8,128)(2,1)}, u32[]{:S(2)}, u32[]{:S(2)}) collective-permute-start(bf16[1,640,512]{2,1,0:T(8,128)(2,1)} %get-tuple-element.1856), channel_id=1, source_target_pairs={{8,0},{16,8},{24,16},{9,1},{17,9},{25,17},{10,2},{18,10},{26,18},{... | collective-permute-start | bytes 1966088 | tf_op jit(solution)/shard_map/while/body/eval_jaxpr/ppermute | solution.py:18
  801.2 6.8 copy-start.3
  811.7 8.7 copy-start.4
  811.7 5.7 copy-start.5
  814.3 6.1 copy-start.14
  833.4 154.9 %collective-permute-start = (bf16[1,640,512]{2,1,0:T(8,128)(2,1)}, bf16[1,640,512]{2,1,0:T(8,128)(2,1)}, u32[]{:S(2)}, u32[]{:S(2)}) collective-permute-start(bf16[1,640,512]{2,1,0:T(8,128)(2,1)} %get-tuple-element.1856), channel_id=1, source_target_pairs={{8,0},{16,8},{24,16},{9,1},{17,9},{25,17},{10,2},{18,10},{26,18},{... | collective-permute-start | bytes 1966088 | tf_op jit(solution)/shard_map/while/body/eval_jaxpr/ppermute | solution.py:18
  836.7 6.8 copy-start.3
  843.4 3.8 copy-start.13
  847.1 8.7 copy-start.4
  847.2 5.7 copy-start.5
  849.8 6.1 copy-start.14
  855.9 134.7 %copy-start.6 = (f32[512,1536]{1,0:T(8,128)}, f32[512,1536]{1,0:T(8,128)S(1)}, u32[]{:S(2)}) copy-start(f32[512,1536]{1,0:T(8,128)S(1)} %select_add_fusion.11) | copy-start | bytes 9437188 | tf_op jit(solution)/shard_map/while
  1122.0 23.7 %collective-permute-start = (bf16[1,640,512]{2,1,0:T(8,128)(2,1)}, bf16[1,640,512]{2,1,0:T(8,128)(2,1)}, u32[]{:S(2)}, u32[]{:S(2)}) collective-permute-start(bf16[1,640,512]{2,1,0:T(8,128)(2,1)} %get-tuple-element.1856), channel_id=1, source_target_pairs={{8,0},{16,8},{24,16},{9,1},{17,9},{25,17},{10,2},{18,10},{26,18},{... | collective-permute-start | bytes 1966088 | tf_op jit(solution)/shard_map/while/body/eval_jaxpr/ppermute | solution.py:18
  1125.3 6.8 copy-start.3
  1135.7 9.8 copy-start.4
  1135.8 6.8 copy-start.5
  1138.4 7.2 copy-start.14
  1279.9 23.7 %collective-permute-start = (bf16[1,640,512]{2,1,0:T(8,128)(2,1)}, bf16[1,640,512]{2,1,0:T(8,128)(2,1)}, u32[]{:S(2)}, u32[]{:S(2)}) collective-permute-start(bf16[1,640,512]{2,1,0:T(8,128)(2,1)} %get-tuple-element.1856), channel_id=1, source_target_pairs={{8,0},{16,8},{24,16},{9,1},{17,9},{25,17},{10,2},{18,10},{26,18},{... | collective-permute-start | bytes 1966088 | tf_op jit(solution)/shard_map/while/body/eval_jaxpr/ppermute | solution.py:18
  1283.1 6.8 copy-start.3
  1293.6 9.9 copy-start.4
  1293.6 6.9 copy-start.5
  1296.2 7.3 copy-start.14
  1437.7 23.6 %collective-permute-start = (bf16[1,640,512]{2,1,0:T(8,128)(2,1)}, bf16[1,640,512]{2,1,0:T(8,128)(2,1)}, u32[]{:S(2)}, u32[]{:S(2)}) collective-permute-start(bf16[1,640,512]{2,1,0:T(8,128)(2,1)} %get-tuple-element.1856), channel_id=1, source_target_pairs={{8,0},{16,8},{24,16},{9,1},{17,9},{25,17},{10,2},{18,10},{26,18},{... | collective-permute-start | bytes 1966088 | tf_op jit(solution)/shard_map/while/body/eval_jaxpr/ppermute | solution.py:18
  1441.0 6.8 copy-start.3
  1451.5 9.9 copy-start.4
  1451.5 6.8 copy-start.5
  1454.1 7.3 copy-start.14
  1595.6 23.6 %collective-permute-start = (bf16[1,640,512]{2,1,0:T(8,128)(2,1)}, bf16[1,640,512]{2,1,0:T(8,128)(2,1)}, u32[]{:S(2)}, u32[]{:S(2)}) collective-permute-start(bf16[1,640,512]{2,1,0:T(8,128)(2,1)} %get-tuple-element.1856), channel_id=1, source_target_pairs={{8,0},{16,8},{24,16},{9,1},{17,9},{25,17},{10,2},{18,10},{26,18},{... | collective-permute-start | bytes 1966088 | tf_op jit(solution)/shard_map/while/body/eval_jaxpr/ppermute | solution.py:18
  1598.8 6.8 copy-start.3
  1609.3 9.8 copy-start.4
  1609.4 6.8 copy-start.5
  1611.9 7.2 copy-start.14
  1622.2 5.8 copy-start.7
  1622.3 5.8 copy-start.38
  1634.6 155.5 %reduce-scatter.9.cloned.1.call-start = ((), (), s32[]{:S(2)}) async-start(), calls=%async_computation.7 | async-start | bytes 327680 | tf_op jit(solution)/shard_map/reduce_scatter | solution.py:362
  1638.0 250.1 %all-reduce.10.cloned.1.call-start = ((), (), s32[]{:S(2)}) async-start(), calls=%async_computation.10 | async-start | bytes 8388608 | tf_op jit(solution)/shard_map/psum | solution.py:23
  1706.8 181.3 %copy-start.31 = (s32[4,640]{1,0:T(4,128)S(1)}, s32[4,640]{1,0:T(4,128)}, u32[]{:S(2)}) copy-start(s32[4,640]{1,0:T(4,128)} %param.34) | copy-start | bytes 30724
  1706.8 181.3 %copy-start.45 = (s32[64]{0:T(128)S(1)}, s32[64]{0:T(128)}, u32[]{:S(2)}) copy-start(s32[64]{0:T(128)} %copy-done.44) | copy-start | bytes 772
  1707.7 183.8 %reduce-scatter.7.cloned.1.call-start = ((), (), s32[]{:S(2)}) async-start(), calls=%async_computation.6 | async-start | bytes 1638400 | tf_op jit(solution)/shard_map/reduce_scatter | solution.py:359
  1708.4 215.7 %reduce-scatter.13.cloned.1.call-start = ((), (), s32[]{:S(2)}) async-start(), calls=%async_computation.9 | async-start | bytes 294912
  1890.5 3.9 copy-start.24
  1894.4 31.0 %copy-start.48 = (bf16[4]{0:T(256)(128)(2,1)S(1)}, bf16[4]{0:T(256)(128)(2,1)}, u32[]{:S(2)}) copy-start(bf16[4]{0:T(256)(128)(2,1)} %copy-done.47) | copy-start | bytes 28
  1894.4 46.9 %copy-start.1 = (f32[2,256,512]{2,1,0:T(8,128)S(1)}, f32[2,256,512]{2,1,0:T(8,128)}, u32[]{:S(2)}) copy-start(f32[2,256,512]{2,1,0:T(8,128)} %param.41) | copy-start | bytes 3145732
  (149 other events, 337.3 us)
Sparse Core Ops, SparseCore 0:
  25.1 108.5 all-reduce.7
  1707.8 180.2 all-reduce.9
Sparse Core Ops, SparseCore 1:
  29.3 36.8 all-gather.1
  1634.7 70.3 reduce-scatter.10
  1707.8 82.2 reduce-scatter.8
  1792.4 87.7 reduce-scatter.6
  1891.5 32.6 reduce-scatter.12
where the time goes:
time: 1960 us; the launch traced here: 1950 us
  waiting for transfers between devices  646 us (33%)
  matrix products  607 us (31%)
  other arithmetic  292 us (15%)
  local copies, waits for them, and re-layouts  236 us (12%)
  starting transfers between devices  104 us (5%)
  blocking collectives  39.8 us (2%)
    dot_general x480, matrix products, product(): return jnp.dot(left, right, preferred_element_type=jnp.float32)  529 us
    ppermute x14, waiting for transfers between devices, shifted_2(): return lax.ppermute(block, axis, route)  289 us
    add x35, other arithmetic, backward_tick(): grad_sums = jax.tree.map(jnp.add, grad_sums, increments)  115 us
    ppermute x14, starting transfers between devices, shifted_2(): return lax.ppermute(block, axis, route)  104 us
    psum x1, waiting for transfers between devices, spread(): return lax.psum(block, axis)  98 us
    psum x1, waiting for transfers between devices, body(): embedded = lax.psum(partial_value, 'section').astype(jnp.float32)  82.7 us
    reduce_scatter x1, waiting for transfers between devices, body(): lax.psum_scatter(table_full.astype(jnp.bfloat16), 'section', scatter_dime...  81 us
    reduce_scatter x1, waiting for transfers between devices, body(): lax.psum_scatter(grad_block, 'dp', scatter_dimension=0, tiled=True)  67 us
  transfers between devices with their start and end apart: 21, of which 14 were waited for; matrix products, arithmetic and copies ran while one was open for 10% of the time, Pallas kernels for 0%

commit v1 on v0

v1 whole, which is shorter than its diff:
```python
import functools

import jax
import jax.numpy as jnp
from jax import lax
from jax.experimental import pallas as pl
from jax.experimental.pallas import tpu as pltpu
from jax.sharding import PartitionSpec as P

D = 512
HEADS = 8
HD = 64
FF = 2048
VOCAB = 256
BAND = 30
LEN = 640
LAYERS = 2
CH = 128
CHUNKS = LEN // CH
REACH = 32
TILE = 512
F32 = jnp.float32
BF16 = jnp.bfloat16


def mm(left, right):
    return jnp.dot(left, right, preferred_element_type=F32)


def mm_nt(left, right):
    return lax.dot_general(left, right, (((1,), (1,)), ((), ())), preferred_element_type=F32)


def norm_forward(v, gain):
    scale = lax.rsqrt(jnp.mean(v * v, axis=-1, keepdims=True) + 1e-05)
    return v * scale * gain


def norm_backward(v, gain, dy):
    scale = lax.rsqrt(jnp.mean(v * v, axis=-1, keepdims=True) + 1e-05)
    normed = v * scale
    dgain = jnp.sum(dy * normed, axis=0, keepdims=True)
    dyg = dy * gain
    dv = scale * (dyg - normed * jnp.mean(dyg * normed, axis=-1, keepdims=True))
    return dv, dgain


def gelu_parts(u):
    c = 0.7978845608028654
    square = u * u
    t = jnp.tanh(u * (c + (c * 0.044715) * square))
    half = 0.5 * (1.0 + t)
    value = u * half
    slope = half + 0.5 * u * (1.0 - t * t) * (c + (3.0 * c * 0.044715) * square)
    return value, slope


def feature_parts(u):
    low_exp = jnp.exp(jnp.minimum(u, 0.0))
    first = jnp.where(u > 0.0, u + 1.0, low_exp)
    second = jnp.tanh(u)
    return first, low_exp, second


def iotas(rows, cols, row0=0):
    r = lax.broadcasted_iota(jnp.int32, (rows, cols), 0) + row0
    c = lax.broadcasted_iota(jnp.int32, (rows, cols), 1)
    return r, c


def near_part(i, key_rows, query_cols):
    row0 = -REACH if i > 0 else 0
    scores = mm(key_rows, query_cols) * 0.125
    r, c = iotas(CH - row0, CH, row0)
    ok = (r <= c) & (c - r < BAND)
    scores = jnp.where(ok, scores, -1e30)
    peak = jnp.max(scores, axis=0, keepdims=True)
    weights = jnp.exp(scores - peak)
    return weights / jnp.sum(weights, axis=0, keepdims=True)


def causal_rows(i, block):
    row0 = -REACH if i > 0 else 0
    r, c = iotas(CH - row0, CH, row0)
    return jnp.where(r <= c, block, 0.0)


def mixture_chunk(i, key_nat, key_feat2, query_masked, query_feat2):
    t0, t1 = i * CH, (i + 1) * CH
    r0 = t0 - REACH if i > 0 else 0
    far = mm(key_feat2[:t1], query_feat2[:, t0:t1])
    near = near_part(i, key_nat[r0:t1], query_masked[:, t0:t1])
    bottom = (causal_rows(i, far[r0:]) + near).astype(BF16)
    if r0 == 0:
        return bottom, near
    return jnp.concatenate([far[:r0].astype(BF16), bottom], axis=0), near


def query_features(qT, inv1, inv2):
    first, slope1, second = feature_parts(qT.astype(F32))
    first_b, second_b = first.astype(BF16), second.astype(BF16)
    scaled = jnp.concatenate([first_b.astype(F32) * inv1, second_b.astype(F32) * inv2], axis=0)
    high = scaled.astype(BF16)
    rest = (scaled - high.astype(F32)).astype(BF16)
    return first_b, slope1, second, jnp.concatenate([high, rest], axis=0)


def masked_pair(part, e):
    zero = jnp.zeros_like(part)
    return jnp.concatenate([part, zero] if e == 0 else [zero, part], axis=0)


def step_kernel(
    tok_ref, tgt_ref, val_ref, table_ref, gm_ref, gf_ref, gz_ref, wm_ref, wo_ref, we_ref, wr_ref,
    loss_ref, lg_ref, dtable_ref, dgm_ref, dgf_ref, dgz_ref, dwm_ref, dwo_ref, dwe_ref, dwrt_ref,
    x_ref, x1_ref, dx_ref, kv_ref, pT_ref, kf_ref, inv1_ref, cum_ref, oT_ref, hT_ref, g_ref, gT_ref,
    wide_ref, a1k_ref, m_ref, d_ref, ds_ref, doT_ref, do_ref, dpT_ref, part_ref, w_ref, yb_ref, acc_ref,
    stage_ref, sem_ref,
):
    inv2 = 1.0 / (lax.broadcasted_iota(jnp.int32, (1, LEN), 1).astype(F32) + 1.0)

    def emit(slot, wait_first, value, dst):
        def copy():
            return pltpu.make_async_copy(stage_ref.at[slot], dst, sem_ref.at[slot])

        if wait_first is True:
            copy().wait()
        elif wait_first is not False:
            pl.when(wait_first)(lambda: copy().wait())
        stage_ref[slot] = value.astype(BF16)
        copy().start()

    vocab_ids = lax.broadcasted_iota(jnp.int32, (LEN, VOCAB), 1)
    hot = (vocab_ids == tok_ref[...]).astype(F32).astype(BF16)
    x_ref[0] = mm_nt(hot, table_ref[...])
    r, c = iotas(LEN, LEN)
    upper = (r <= c).astype(F32).astype(BF16)
    wide_ref[...] = upper

    def attention_forward(l):
        x = x_ref[l]
        h = norm_forward(x, gm_ref[l]).astype(BF16)
        hT_ref[l] = h.T
        for j in range(3):
            part = mm(h, wm_ref[l, :, j * TILE:(j + 1) * TILE]).astype(BF16)
            if j > 0:
                kv_ref[l, :, (j - 1) * TILE:j * TILE] = part
            pT_ref[l, j * TILE:(j + 1) * TILE, :] = part.T
        kT = pT_ref[l, D:2 * D, :].astype(F32)
        a1k_ref[...] = feature_parts(kT)[0].astype(BF16)
        for i in range(CHUNKS):
            t0, t1 = i * CH, (i + 1) * CH
            cum_ref[l, :, t0:t1] = mm(a1k_ref[:, :t1], wide_ref[:t1, t0:t1])

        def pair(p, carry):
            base = pl.multiple_of(p * CH, CH)
            for e in range(2):
                row = pl.multiple_of(base + e * HD, HD)
                qT = pT_ref[l, pl.ds(row, HD), :]
                kT = pT_ref[l, pl.ds(pl.multiple_of(D + row, HD), HD), :]
                vT = pT_ref[l, pl.ds(pl.multiple_of(2 * D + row, HD), HD), :]
                first_k, _, second_k = feature_parts(kT.astype(F32))
                key_feat = jnp.concatenate([first_k.astype(BF16), second_k.astype(BF16)], axis=0).T
                kf_ref[l, :, pl.ds(pl.multiple_of(2 * row, CH), CH)] = key_feat
                first_q = feature_parts(qT.astype(F32))[0].astype(BF16).astype(F32)
                total = jnp.sum(first_q * cum_ref[l, pl.ds(row, HD), :], axis=0, keepdims=True)
                inv1 = 1.0 / (total + 1.0)
                inv1_ref[l, 2 * p + e] = inv1
                query_feat2 = query_features(qT, inv1, inv2)[3]
                key_feat2 = jnp.concatenate([key_feat, key_feat], axis=1)
                key_nat = kv_ref[l, :, pl.ds(base, CH)]
                query_masked = masked_pair(qT, e)
                for i in range(CHUNKS):
                    t0, t1 = i * CH, (i + 1) * CH
                    mixture, _ = mixture_chunk(i, key_nat, key_feat2, query_masked, query_feat2)
                    oT_ref[l, pl.ds(row, HD), t0:t1] = mm(vT[:, :t1], mixture).astype(BF16)
            return carry

        lax.fori_loop(0, HEADS // 2, pair, 0)
        o = oT_ref[l].T
        x1_ref[l] = x_ref[l] + mm(o, wo_ref[l])

    def feed_forward(l):
        x1 = x1_ref[l]
        g_ref[l] = norm_forward(x1, gf_ref[l]).astype(BF16)
        gT_ref[l] = g_ref[l].T
        x_ref[l + 1] = x1

        def tile(j, carry):
            col = pl.multiple_of(j * TILE, TILE)
            active = gelu_parts(mm(g_ref[l], we_ref[l, :, pl.ds(col, TILE)]))[0].astype(BF16)
            x_ref[l + 1] += mm(active, wr_ref[l, pl.ds(col, TILE), :])
            return carry

        lax.fori_loop(0, FF // TILE, tile, 0)

    def head():
        x = x_ref[LAYERS]
        z = norm_forward(x, gz_ref[...]).astype(BF16)
        logits = mm(z, table_ref[...])
        tgt_hot = (vocab_ids == tgt_ref[...]).astype(F32)
        val = val_ref[...]
        peak = jnp.max(logits, axis=-1, keepdims=True)
        grown = jnp.exp(logits - peak)
        total = jnp.sum(grown, axis=-1, keepdims=True)
        lse = peak + jnp.log(total)
        picked = jnp.sum(logits * tgt_hot, axis=-1, keepdims=True)
        cross = (lse - picked) * val
        loss = jnp.sum(cross, axis=0, keepdims=True) / jnp.sum(val, axis=0, keepdims=True)
        loss_ref[...] = jnp.broadcast_to(loss, loss_ref.shape)
        grad_b = ((grown / total - tgt_hot) * val).astype(BF16)
        lg_ref[...] = grad_b
        dtable_ref[...] = mm(z.T, grad_b)
        dv, dgain = norm_backward(x, gz_ref[...], mm_nt(grad_b, table_ref[...]))
        dgz_ref[...] = dgain
        dx_ref[...] = dv

    def feed_backward(l):
        yb = dx_ref[...].astype(BF16)
        yb_ref[...] = yb
        ybT = yb.T
        doT_ref[...] = ybT
        acc_ref[...] = jnp.zeros_like(acc_ref)

        def tile(j, carry):
            col = pl.multiple_of(j * TILE, TILE)
            slot = lax.rem(j, 2)
            later = (j >= 2) if l == LAYERS - 1 else True
            value, slope = gelu_parts(mm(g_ref[l], we_ref[l, :, pl.ds(col, TILE)]))
            emit(slot, later, mm(doT_ref[...], value.astype(BF16)), dwrt_ref.at[l, :, pl.ds(col, TILE)])
            dact = mm_nt(yb_ref[...], wr_ref[l, pl.ds(col, TILE), :])
            dhid = (dact * slope).astype(BF16)
            emit(2 + slot, later, mm(gT_ref[l], dhid), dwe_ref.at[l, :, pl.ds(col, TILE)])
            acc_ref[...] += mm_nt(dhid, we_ref[l, :, pl.ds(col, TILE)])
            return carry

        lax.fori_loop(0, FF // TILE, tile, 0)
        dv, dgain = norm_backward(x1_ref[l], gf_ref[l], acc_ref[...])
        dgf_ref[l] = dgain
        dx_ref[...] += dv

    def attention_backward(l):
        yb = dx_ref[...].astype(BF16)
        yb_ref[...] = yb
        emit(0, True, mm(oT_ref[l], yb), dwo_ref.at[l])
        do_ref[...] = mm_nt(yb, wo_ref[l]).astype(BF16)
        doT_ref[...] = do_ref[...].T

        def pair(p, carry):
            base = pl.multiple_of(p * CH, CH)
            for e in range(2):
                row = pl.multiple_of(base + e * HD, HD)
                qT = pT_ref[l, pl.ds(row, HD), :]
                kT = pT_ref[l, pl.ds(pl.multiple_of(D + row, HD), HD), :]
                doT = doT_ref[pl.ds(row, HD), :]
                inv1 = inv1_ref[l, 2 * p + e]
                first_q, slope1_q, second_q, query_feat2 = query_features(qT, inv1, inv2)
                first_k, slope1_k, second_k = feature_parts(kT.astype(F32))
                key_featT = jnp.concatenate([first_k.astype(BF16), second_k.astype(BF16)], axis=0)
                key_feat = kf_ref[l, :, pl.ds(pl.multiple_of(2 * row, CH), CH)]
                key_feat2 = jnp.concatenate([key_feat, key_feat], axis=1)
                key_nat = kv_ref[l, :, pl.ds(base, CH)]
                value_nat = kv_ref[l, :, pl.ds(pl.multiple_of(D + base, CH), CH)]
                query_masked = masked_pair(qT, e)
                do_masked = masked_pair(doT, e)
                far_q, near_q = [], []
                for i in range(CHUNKS):
                    t0, t1 = i * CH, (i + 1) * CH
                    r0 = t0 - REACH if i > 0 else 0
                    mixture, near = mixture_chunk(i, key_nat, key_feat2, query_masked, query_feat2)
                    m_ref[e, :t1, t0:t1] = mixture
                    dm = mm(value_nat[:t1], do_masked[:, t0:t1])
                    bottom = dm[r0:]
                    dm_b = causal_rows(i, bottom).astype(BF16)
                    if r0 > 0:
                        dm_b = jnp.concatenate([dm[:r0].astype(BF16), dm_b], axis=0)
                    d_ref[e, :t1, t0:t1] = dm_b
                    weighted = near * bottom
                    dsum = jnp.sum(weighted, axis=0, keepdims=True)
                    ds = ((weighted - near * dsum) * 0.125).astype(BF16)
                    far_q.append(mm(key_featT[:, :t1], dm_b))
                    if i > 0:
                        before = jnp.concatenate([jnp.zeros((CH - REACH, CH), BF16), ds[:REACH]], axis=0)
                        ds_ref[e, t0 - CH:t0, CH:] = before
                        ds = ds[REACH:]
                        near_q.append(mm(kT[:, t0 - CH:t1], jnp.concatenate([before, ds], axis=0)))
                    else:
                        near_q.append(mm(kT[:, t0:t1], ds))
                    ds_ref[e, t0:t1, :CH] = ds
                farT = jnp.concatenate(far_q, axis=1)
                y1, y2 = farT[:HD], farT[HD:]
                first_qf = first_q.astype(F32)
                m = inv1 * jnp.sum(first_qf * y1, axis=0, keepdims=True)
                cum = cum_ref[l, pl.ds(row, HD), :]
                dq = jnp.concatenate(near_q, axis=1)
                dq = dq + (inv1 * (y1 - m * cum)) * slope1_q + (inv2 * y2) * (1.0 - second_q * second_q)
                dpT_ref[pl.ds(row, HD), :] = dq.astype(BF16)
                w_ref[pl.ds(row, HD), :] = (first_qf * (m * inv1)).astype(BF16)
                for i in range(CHUNKS):
                    t0, t1 = i * CH, (i + 1) * CH
                    far = mm_nt(query_feat2[:, t0:], d_ref[e, t0:t1, t0:])
                    far = far[:CH] + far[CH:]
                    t2 = min(t1 + CH, LEN)
                    near = mm_nt(qT[:, t0:t2], ds_ref[e, t0:t1, :t2 - t0])
                    dk = near + far[:HD] * slope1_k[:, t0:t1]
                    dk = dk + far[HD:] * (1.0 - second_k[:, t0:t1] * second_k[:, t0:t1])
                    part_ref[pl.ds(row, HD), t0:t1] = dk
                    dv = mm_nt(doT[:, t0:], m_ref[e, t0:t1, t0:])
                    dpT_ref[pl.ds(pl.multiple_of(2 * D + row, HD), HD), t0:t1] = dv.astype(BF16)
            return carry

        lax.fori_loop(0, HEADS // 2, pair, 0)
        kT = pT_ref[l, D:2 * D, :].astype(F32)
        slope1_k = jnp.exp(jnp.minimum(kT, 0.0))
        for i in range(CHUNKS):
            t0, t1 = i * CH, (i + 1) * CH
            back = mm_nt(w_ref[:, t0:], wide_ref[t0:t1, t0:])
            dk = part_ref[:, t0:t1] - back * slope1_k[:, t0:t1]
            dpT_ref[D:2 * D, t0:t1] = dk.astype(BF16)
        for j in range(3):
            tile = mm_nt(hT_ref[l], dpT_ref[j * TILE:(j + 1) * TILE, :])
            emit(1 + j, True, tile, dwm_ref.at[l, :, j * TILE:(j + 1) * TILE])
        dh = mm(wm_ref[l], dpT_ref[...]).T
        dv, dgain = norm_backward(x_ref[l], gm_ref[l], dh)
        dgm_ref[l] = dgain
        dx_ref[...] += dv

    for l in range(LAYERS):
        attention_forward(l)
        feed_forward(l)
    head()
    for l in reversed(range(LAYERS)):
        feed_backward(l)
        attention_backward(l)
    dtable_ref[...] += mm(dx_ref[...].astype(BF16).T, hot)
    for slot in range(4):
        pltpu.make_async_copy(stage_ref.at[slot], dwo_ref.at[0], sem_ref.at[slot]).wait()


def local_step(tok, tgt, val, table, gm, gf, gz, wm, wo, we, wr):
    vmem = pl.BlockSpec(memory_space=pltpu.VMEM)
    hbm = pl.BlockSpec(memory_space=pl.ANY)
    shape = jax.ShapeDtypeStruct
    return pl.pallas_call(
        step_kernel,
        out_shape=(
            shape((8, 128), F32),
            shape((LEN, VOCAB), BF16),
            shape((D, VOCAB), F32),
            shape((LAYERS, 1, D), F32),
            shape((LAYERS, 1, D), F32),
            shape((1, D), F32),
            shape((LAYERS, D, 3 * D), BF16),
            shape((LAYERS, D, D), BF16),
            shape((LAYERS, D, FF), BF16),
            shape((LAYERS, D, FF), BF16),
        ),
        in_specs=[vmem] * 11,
        out_specs=(vmem,) * 6 + (hbm,) * 4,
        scratch_shapes=[
            pltpu.VMEM((LAYERS + 1, LEN, D), F32),
            pltpu.VMEM((LAYERS, LEN, D), F32),
            pltpu.VMEM((LEN, D), F32),
            pltpu.VMEM((LAYERS, LEN, 2 * D), BF16),
            pltpu.VMEM((LAYERS, 3 * D, LEN), BF16),
            pltpu.VMEM((LAYERS, LEN, 2 * D), BF16),
            pltpu.VMEM((LAYERS, HEADS, 1, LEN), F32),
            pltpu.VMEM((LAYERS, D, LEN), F32),
            pltpu.VMEM((LAYERS, D, LEN), BF16),
            pltpu.VMEM((LAYERS, D, LEN), BF16),
            pltpu.VMEM((LAYERS, LEN, D), BF16),
            pltpu.VMEM((LAYERS, D, LEN), BF16),
            pltpu.VMEM((LEN, LEN), BF16),
            pltpu.VMEM((D, LEN), BF16),
            pltpu.VMEM((2, LEN, LEN), BF16),
            pltpu.VMEM((2, LEN, LEN), BF16),
            pltpu.VMEM((2, LEN, 2 * CH), BF16),
            pltpu.VMEM((D, LEN), BF16),
            pltpu.VMEM((LEN, D), BF16),
            pltpu.VMEM((3 * D, LEN), BF16),
            pltpu.VMEM((D, LEN), F32),
            pltpu.VMEM((D, LEN), BF16),
            pltpu.VMEM((LEN, D), BF16),
            pltpu.VMEM((LEN, D), F32),
            pltpu.VMEM((4, D, TILE), BF16),
            pltpu.SemaphoreType.DMA((4,)),
        ],
        compiler_params=pltpu.CompilerParams(vmem_limit_bytes=63 * 1024 * 1024),
        cost_estimate=pl.CostEstimate(flops=40_000_000_000, bytes_accessed=40_000_000, transcendentals=0),
        name="local_step",
    )(tok, tgt, val, table, gm, gf, gz, wm, wo, we, wr)


def body(
    tokens,
    padding_mask,
    embedding,
    mixer_weight,
    output_weight,
    mixer_gain,
    expand_weight,
    reduce_weight,
    feed_gain,
    final_gain,
):
    segments = lax.axis_size("section")
    segment_index = lax.axis_index("section")
    item_count = tokens.shape[0]
    assert item_count == segments
    slice_width = embedding.shape[1]

    token_row = lax.dynamic_index_in_dim(tokens, segment_index, 0, keepdims=False)
    mask_row = lax.dynamic_index_in_dim(padding_mask, segment_index, 0, keepdims=False)
    target_row = jnp.concatenate([token_row[1:], jnp.zeros((1,), jnp.int32)])
    valid_row = jnp.concatenate([mask_row[1:], jnp.zeros((1,), jnp.int32)]).astype(F32)

    def gather(block, dim):
        return lax.all_gather(block.astype(BF16), "dp", axis=dim, tiled=True)

    table = lax.all_gather(gather(embedding, 0), "section", axis=1, tiled=True)
    gains = gather(jnp.concatenate([mixer_gain, feed_gain, final_gain[None]], axis=0), 1).astype(F32)
    wm = gather(mixer_weight, 1)
    wo = gather(output_weight, 1)
    we = gather(expand_weight, 1)
    wr = gather(reduce_weight, 1)
    loss, lg, dtable, dgm, dgf, dgz, dwm, dwo, dwe, dwrt = local_step(
        token_row[:, None], target_row[:, None], valid_row[:, None], table,
        gains[0:2, None], gains[2:4, None], gains[4:5], wm, wo, we, wr,
    )
    item_loss = lax.all_gather(loss[0, 0], "section")
    parts = lg.reshape(LEN, segments, slice_width).transpose(1, 0, 2)
    logit_grad = lax.all_to_all(parts, "section", 0, 0, tiled=True).astype(F32)

    def shard(grad, dim):
        part = lax.psum_scatter(grad.astype(BF16), "dp", scatter_dimension=dim, tiled=True)
        return lax.psum(part, "section").astype(F32)

    table_part = lax.psum_scatter(dtable.astype(BF16), "dp", scatter_dimension=0, tiled=True)
    table_grad = lax.psum_scatter(table_part, "section", scatter_dimension=1, tiled=True).astype(F32)
    gain_grads = lax.psum_scatter(
        jnp.concatenate([dgm[:, 0], dgf[:, 0], dgz], axis=0), "dp", scatter_dimension=1, tiled=True
    )
    gain_grads = lax.psum(gain_grads, "section")
    return (
        item_loss,
        logit_grad,
        table_grad,
        shard(dwm, 1),
        shard(dwo, 1),
        gain_grads[0:2],
        shard(dwe, 1),
        jnp.swapaxes(shard(dwrt, 2), 1, 2),
        gain_grads[2:4],
        gain_grads[4],
    )


def solution(mesh):
    placed = (
        P("dp", None),
        P("dp", None),
        P("dp", "section"),
        P(None, "dp", None),
        P(None, "dp", None),
        P(None, "dp"),
        P(None, "dp", None),
        P(None, "dp", None),
        P(None, "dp"),
        P("dp"),
    )
    return jax.shard_map(
        body,
        mesh=mesh,
        in_specs=placed,
        out_specs=(
            P("dp"),
            P("dp", None, "section"),
            P("dp", "section"),
            P(None, "dp", None),
            P(None, "dp", None),
            P(None, "dp"),
            P(None, "dp", None),
            P(None, "dp", None),
            P(None, "dp"),
            P("dp"),
        ),
        check_vma=False,
    )
```

time: 1960 us -> 649 us (0.33)
  matrix products: 607 us -> 0 us
  other arithmetic: 292 us -> 14.9 us
  local copies, waits for them, and re-layouts: 236 us -> 17.7 us
  waiting for transfers between devices: 646 us -> 431 us
  Pallas kernels: 0 us -> 115 us
  starting transfers between devices: 104 us -> 5.09 us
    dot_general x510 -> x0, matrix products: 607 us -> none  [the longest x480 529 us: product(): return jnp.dot(left, right, preferred_element_type=jnp.float32)]
    ppermute x14 -> x0, waiting for transfers between devices: 289 us -> none  [shifted_2(): return lax.ppermute(block, axis, route)]
    add x136 -> x0, other arithmetic: 122 us -> none  [the longest x35 115 us: backward_tick(): grad_sums = jax.tree.map(jnp.add, grad_sums, increments)]
    pallas_call x0 -> x1, Pallas kernels: none -> 115 us  [local_step(): pl.pallas_call(step_kernel, out_shape=(shape((8, 128), F32), shape((LEN,...]
    psum x2 -> x1, waiting for transfers between devices: 181 us -> 68.6 us  [shard(): return lax.psum(part, 'section').astype(F32)]
    ppermute x14 -> x0, starting transfers between devices: 104 us -> none  [shifted_2(): return lax.ppermute(block, axis, route)]
    all_gather x1 -> x4, waiting for transfers between devices: 0.01 us -> 95 us  [gather(): return lax.all_gather(block.astype(BF16), 'dp', axis=dim, tiled=True)]
    reduce_scatter x3 -> x5, waiting for transfers between devices: 148 us -> 228 us  [the longest x4 198 us: shard(): lax.psum_scatter(grad.astype(BF16), 'dp', scatter_dimension=dim, tiled=True)]
  transfers between devices with their start and end apart: 21 -> 13, of which waited for: 14 -> 11; matrix products, arithmetic and copies ran while one was open for 10% -> 3% of each run, Pallas kernels for 0% -> 0%
where the time goes in v1:
time: 649 us; the launch traced here: 645 us
  waiting for transfers between devices  431 us (66%)
  Pallas kernels  115 us (18%)
  blocking collectives  46 us (7%)
  local copies, waits for them, and re-layouts  17.7 us (3%)
  other arithmetic  14.9 us (2%)
  between operations  14.9 us (2%)
    reduce_scatter x4, waiting for transfers between devices, shard(): lax.psum_scatter(grad.astype(BF16), 'dp', scatter_dimension=dim, tiled=True)  198 us
    pallas_call x1, Pallas kernels, local_step(): pl.pallas_call(step_kernel, out_shape=(shape((8, 128), F32), shape((LEN,...  115 us
    all_gather x4, waiting for transfers between devices, gather(): return lax.all_gather(block.astype(BF16), 'dp', axis=dim, tiled=True)  95 us
    psum x1, waiting for transfers between devices, shard(): return lax.psum(part, 'section').astype(F32)  68.6 us
    unnamed x14, waiting for transfers between devices  38.9 us
    reduce_scatter x1, waiting for transfers between devices, body(): lax.psum_scatter(dtable.astype(BF16), 'dp', scatter_dimension=0, tiled=True)  29.9 us
    all_gather x2, blocking collectives, gather(): return lax.all_gather(block.astype(BF16), 'dp', axis=dim, tiled=True)  19.5 us
    all_gather x1, blocking collectives, body(): table = lax.all_gather(gather(embedding, 0), 'section', axis=1, tiled=True)  14.1 us
  transfers between devices with their start and end apart: 13, of which 11 were waited for; matrix products, arithmetic and copies ran while one was open for 3% of the time, Pallas kernels for 0%

profile of v1, /device:TPU:0, one launch (start us, length us, event | category | flops | bytes accessed | tf_op | source)
XLA Modules:
  0.0 644.6 jit_solution(18319612382839122714)
XLA Ops:
  7.2 0.0 all-gather.9.cloned.1.call-start
  7.3 1.7 convert_element_type.52
  9.0 0.0 all-gather.7.cloned.1.call-start
  9.0 1.9 convert_element_type.51
  11.0 0.0 all-gather.11.cloned.1.call-start
  11.0 2.1 convert_element_type.53
  13.1 0.0 all-gather.13.cloned.1.call-start
  13.2 0.9 convert_element_type.54
  14.1 0.0 reduce-scatter.12.cloned.1.call-start
  14.2 0.8 dynamic-slice_bitcast_fusion
  15.0 0.1 pad_add_fusion
  15.0 0.9 broadcast_in_dim.22.tgt_ref
  15.9 0.1 add_convert_fusion
  16.0 0.9 copy.57.val_ref
  16.9 0.9 copy.55.tok_ref
  17.9 10.4 %all-gather.1 = bf16[8,64,5]{1,2,0:T(8,128)(2,1)S(1)} all-gather(bf16[1,64,5]{1,2,0:T(8,128)(2,1)S(1)} %maximum_bitcast_fusion), channel_id=1, replica_groups=mesh['section'=4,'dp'=8] {'dp'}, dimensions={0}, use_global_device_ids=true | all-gather | bytes 5760 | tf_op jit(solution)/shard_map/all_gather | solution.py:418
  28.3 0.1 reshape.63
  28.3 0.6 slice.43.gz_ref
  28.9 0.6 copy.59.gm_ref
  29.5 0.6 copy.60.gf_ref
  30.1 9.2 %all_gather.24 = bf16[512,64]{1,0:T(8,128)(2,1)S(1)} all-gather(bf16[64,64]{1,0:T(8,128)(2,1)S(1)} %convert_element_type.49), channel_id=1, replica_groups=mesh['section'=4,'dp'=8] {'dp'}, dimensions={0}, use_global_device_ids=true | all-gather | bytes 73728 | tf_op jit(solution)/shard_map/all_gather | solution.py:418
  39.3 0.1 copy.53
  39.4 14.1 %all_gather.25 = bf16[512,256]{0,1:T(8,128)(2,1)S(1)} all-gather(bf16[512,64]{0,1:T(8,128)(2,1)S(1)} %copy.53), channel_id=1, replica_groups=mesh['section'=4,'dp'=8] {'section'}, dimensions={1}, use_global_device_ids=true | all-gather | bytes 327680 | tf_op jit(solution)/shard_map/all_gather | solution.py:420
  53.5 0.8 copy.58.table_ref
  54.4 16.7 %all-gather.7.cloned.1.call-done.wm_ref = bf16[2,512,1536]{2,1,0:T(8,128)(2,1)} async-done(((bf16[2,64,1536]{2,1,0:T(8,128)(2,1)}), bf16[2,512,1536]{2,1,0:T(8,128)(2,1)}) %all-gather.7.cloned.1.call-update) | async-done | bytes 3145744 | tf_op jit(solution)/shard_map/all_gather | solution.py:418
  71.0 39.2 %all-gather.11.cloned.1.call-done.we_ref = bf16[2,512,2048]{2,1,0:T(8,128)(2,1)} async-done(((bf16[2,64,2048]{2,1,0:T(8,128)(2,1)}), bf16[2,512,2048]{2,1,0:T(8,128)(2,1)}) %all-gather.11.cloned.1.call-update) | async-done | bytes 4194320 | tf_op jit(solution)/shard_map/all_gather | solution.py:418
  110.3 39.1 %all-gather.13.cloned.1.call-done.wr_ref = bf16[2,2048,512]{2,1,0:T(8,128)(2,1)} async-done(((bf16[2,256,512]{2,1,0:T(8,128)(2,1)}), bf16[2,2048,512]{2,1,0:T(8,128)(2,1)}) %all-gather.13.cloned.1.call-update) | async-done | bytes 4194320 | tf_op jit(solution)/shard_map/all_gather | solution.py:418
  149.4 115.4 %local_step.1 = (f32[8,128]{1,0:T(8,128)}, bf16[640,256]{1,0:T(8,128)(2,1)}, f32[512,256]{1,0:T(8,128)}, f32[2,1,512]{2,1,0:T(1,128)}, f32[2,1,512]{2,1,0:T(1,12...) custom-call(s32[640,1]{1,0:T(8,128)} %copy.55.tok_ref, ...), custom_call_target="tpu_custom_call" | custom-call | flops 40000000000 | bytes 40000000 | tf_op jit(solution)/shard_map/local_step/pallas_call | solution.py:344
  264.8 1.8 convert_element_type.56
  266.6 0.0 reduce-scatter.16.cloned.1.call-start
  266.7 0.5 reduce-scatter.16.cloned.1.call-update
  267.2 0.7 reduce-scatter.14.cloned.1.call-update
  267.9 0.0 reduce-scatter.20.cloned.1.call-start
  268.0 0.7 reduce-scatter.20.cloned.1.call-update
  268.8 0.7 reduce-scatter.18.cloned.1.call-update
  269.4 0.0 reduce-scatter.24.cloned.1.call-start
  269.6 0.9 copy.65
  270.4 0.0 reduce-scatter.22.cloned.1.call-start
  270.5 29.9 %reduce-scatter.12.cloned.1.call-done = bf16[64,256]{1,0:T(8,128)(2,1)} async-done(((bf16[512,256]{1,0:T(8,128)(2,1)}), bf16[64,256]{1,0:T(8,128)(2,1)}) %reduce-scatter.12.cloned.1.call-update) | async-done | bytes 32784 | tf_op jit(solution)/shard_map/reduce_scatter | solution.py:438
  300.4 1.5 copy.63
  301.9 0.0 all-reduce.5.cloned.1.call-start
  301.9 38.4 %reduce-scatter.16.cloned.1.call-done = bf16[2,64,512]{2,1,0:T(8,128)(2,1)} async-done(((bf16[2,512,512]{2,1,0:T(8,128)(2,1)}), bf16[2,64,512]{2,1,0:T(8,128)(2,1)}) %reduce-scatter.16.cloned.1.call-update) | async-done | bytes 131088 | tf_op jit(solution)/shard_map/reduce_scatter | solution.py:435
  340.4 50.1 %reduce-scatter.14.cloned.1.call-done = bf16[2,64,1536]{2,1,0:T(8,128)(2,1)} async-done(((bf16[2,512,1536]{2,1,0:T(8,128)(2,1)}), bf16[2,64,1536]{2,1,0:T(8,128)(2,1)}) %reduce-scatter.14.cloned.1.call-update) | async-done | bytes 393232 | tf_op jit(solution)/shard_map/reduce_scatter | solution.py:435
  390.4 54.7 %reduce-scatter.20.cloned.1.call-done = bf16[2,512,256]{2,1,0:T(8,128)(2,1)} async-done(((bf16[2,512,2048]{2,1,0:T(8,128)(2,1)}), bf16[2,512,256]{2,1,0:T(8,128)(2,1)}) %reduce-scatter.20.cloned.1.call-update) | async-done | bytes 524304 | tf_op jit(solution)/shard_map/reduce_scatter | solution.py:435
  445.1 55.1 %reduce-scatter.18.cloned.1.call-done = bf16[2,64,2048]{2,1,0:T(8,128)(2,1)} async-done(((bf16[2,512,2048]{2,1,0:T(8,128)(2,1)}), bf16[2,64,2048]{2,1,0:T(8,128)(2,1)}) %reduce-scatter.18.cloned.1.call-update) | async-done | bytes 524304 | tf_op jit(solution)/shard_map/reduce_scatter | solution.py:435
  500.3 0.9 copy.61
  501.2 4.6 all-to-all-start
  505.8 0.6 dynamic-slice
  506.4 1.2 slice.37
  507.5 1.3 bitcast_dynamic-update-slice_fusion
  508.9 28.5 %reduce-scatter.24.cloned.1.call-done = f32[64,5]{1,0:T(8,128)} async-done(((f32[512,5]{1,0:T(8,128)}), f32[64,5]{1,0:T(8,128)}) %reduce-scatter.24.cloned.1.call-update) | async-done | bytes 1296
  537.3 0.8 copy.66
  538.2 12.3 %all-reduce.1 = (f32[4]{0:T(128)}, f32[5,64]{1,0:T(8,128)S(1)}) all-reduce(f32[4]{0:T(128)S(1)} %bitcast_dynamic-update-slice_fusion, f32[5,64]{1,0:T(8,128)S(1)} %copy.66), channel_id=2, replica_groups=mesh['section'=4,'dp'=8] {'section'}, use_global_device_ids=true, to_apply=%add | all-reduce | flops 324 | bytes 2592 | tf_op jit(solution)/shard_map/all_gather | solution.py:430
  550.5 0.5 slice_bitcast_fusion.2
  551.0 0.6 fusion
  551.6 7.7 %reduce-scatter.22.cloned.1.call-done = bf16[64,64]{1,0:T(8,128)(2,1)} async-done(((bf16[256,64]{1,0:T(8,128)(2,1)}), bf16[64,64]{1,0:T(8,128)(2,1)}) %reduce-scatter.22.cloned.1.call-update) | async-done | bytes 8208
  559.3 0.8 copy.64
  560.1 0.6 convert_element_type.57
  560.7 0.9 convert_element_type.55
  561.6 68.6 %all-reduce.5.cloned.1.call-done = (bf16[2,256,512]{1,2,0:T(8,128)(2,1)}, bf16[2,64,1536]{2,1,0:T(8,128)(2,1)}, bf16[2,64,512]{2,1,0:T(8,128)(2,1)}, bf16[2,64,2048]{2,1,0:T(8,128)(2,1)}) async-done(((bf16[2,256,512]{1,2,0:T(8,128)(2,1)}, bf16[2,64,1536]{2,1,0:T(8,128)(2,1)}, bf16[2,64,512]{2,1,0:T(8,128)(2,1)}, bf16[2,64,2048]{2,1,0:T(8,128)(2,1)}), (bf16[2,256,512]{1,2,0:T(8,128)(2,1)}, ...) | async-done | bytes 1572880 | tf_op jit(solution)/shard_map/psum | solution.py:436
  630.2 2.2 convert_element_type.60
  632.4 2.2 copy.62
  634.6 2.0 convert_element_type.58
  636.5 0.7 convert_element_type.59
  (48 shorter events, 0.3 us)
Async XLA Ops:
  7.2 6.0 copy-start
  7.2 7.0 %copy-start.6 = (s32[4,640]{1,0:T(4,128)S(1)}, s32[4,640]{1,0:T(4,128)}, u32[]{:S(2)}) copy-start(s32[4,640]{1,0:T(4,128)} %param.10) | copy-start | bytes 30724
  7.2 10.7 %copy-start.8 = (f32[2,64]{1,0:T(2,128)S(1)}, f32[2,64]{1,0:T(2,128)}, u32[]{:S(2)}) copy-start(f32[2,64]{1,0:T(2,128)} %param.15) | copy-start | bytes 1540
  7.2 10.6 %copy-start.9 = (f32[2,64]{1,0:T(2,128)S(1)}, f32[2,64]{1,0:T(2,128)}, u32[]{:S(2)}) copy-start(f32[2,64]{1,0:T(2,128)} %param.18) | copy-start | bytes 1540
  7.2 10.7 %copy-start.10 = (f32[64]{0:T(128)S(1)}, f32[64]{0:T(128)}, u32[]{:S(2)}) copy-start(f32[64]{0:T(128)} %param.19) | copy-start | bytes 772
  7.2 22.9 %copy-start.3 = (f32[64,64]{1,0:T(8,128)S(1)}, f32[64,64]{1,0:T(8,128)}, u32[]{:S(2)}) copy-start(f32[64,64]{1,0:T(8,128)} %param.12) | copy-start | bytes 49156
  7.2 47.1 %all-gather.9.cloned.1.call-start = ((), (), s32[]{:S(2)}) async-start(), calls=%async_computation.9 | async-start | bytes 1179648 | tf_op jit(solution)/shard_map/all_gather | solution.py:418
  9.0 62.1 %all-gather.7.cloned.1.call-start = ((), (), s32[]{:S(2)}) async-start(), calls=%async_computation.8 | async-start | bytes 3538944 | tf_op jit(solution)/shard_map/all_gather | solution.py:418
  11.0 99.3 %all-gather.11.cloned.1.call-start = ((), (), s32[]{:S(2)}) async-start(), calls=%async_computation.10 | async-start | bytes 4718592 | tf_op jit(solution)/shard_map/all_gather | solution.py:418
  13.1 136.2 %all-gather.13.cloned.1.call-start = ((), (), s32[]{:S(2)}) async-start(), calls=%async_computation.11 | async-start | bytes 4718592 | tf_op jit(solution)/shard_map/all_gather | solution.py:418
  14.1 286.3 %reduce-scatter.12.cloned.1.call-start = ((), (), s32[]{:S(2)}) async-start(), calls=%async_computation.12 | async-start | bytes 294912 | tf_op jit(solution)/shard_map/reduce_scatter | solution.py:438
  266.6 73.8 %reduce-scatter.16.cloned.1.call-start = ((), (), s32[]{:S(2)}) async-start(), calls=%async_computation.14 | async-start | bytes 1179648 | tf_op jit(solution)/shard_map/reduce_scatter | solution.py:435
  267.2 123.2 %reduce-scatter.14.cloned.1.call-start = ((), (), s32[]{:S(2)}) async-start(), calls=%async_computation.13 | async-start | bytes 3538944 | tf_op jit(solution)/shard_map/reduce_scatter | solution.py:435
  267.9 177.2 %reduce-scatter.20.cloned.1.call-start = ((), (), s32[]{:S(2)}) async-start(), calls=%async_computation.16 | async-start | bytes 4718592 | tf_op jit(solution)/shard_map/reduce_scatter | solution.py:435
  268.0 1.5 copy-start.5
  268.0 1.5 copy-start.4
  268.0 1.5 copy-start.7
  268.7 231.6 %copy-start.1 = (bf16[640,256]{1,0:T(8,128)(2,1)S(1)}, bf16[640,256]{1,0:T(8,128)(2,1)}, u32[]{:S(2)}) copy-start(bf16[640,256]{1,0:T(8,128)(2,1)} %get-tuple-element.21) | copy-start | bytes 983044
  268.7 237.1 %copy-start.11 = (u32[32]{0:T(128)S(1)}, u32[32]{0:T(128)}, u32[]{:S(2)}) copy-start(u32[32]{0:T(128)} %constant.21) | copy-start | bytes 388
  268.7 231.5 %reduce-scatter.18.cloned.1.call-start = ((), (), s32[]{:S(2)}) async-start(), calls=%async_computation.15 | async-start | bytes 4718592 | tf_op jit(solution)/shard_map/reduce_scatter | solution.py:435
  269.4 267.9 %reduce-scatter.24.cloned.1.call-start = ((), (), s32[]{:S(2)}) async-start(), calls=%async_computation.18 | async-start | bytes 294912
  270.4 288.9 %reduce-scatter.22.cloned.1.call-start = ((), (), s32[]{:S(2)}) async-start(), calls=%async_computation.17 | async-start | bytes 81920
  301.9 328.3 %all-reduce.5.cloned.1.call-start = ((), (), s32[]{:S(2)}) async-start(), calls=%async_computation.19 | async-start | bytes 3145728 | tf_op jit(solution)/shard_map/psum | solution.py:436
  501.2 59.6 %all-to-all-start = ((bf16[4,640,64]{1,2,0:T(8,128)(2,1)}), bf16[4,640,64]{1,2,0:T(8,128)(2,1)S(1)}, u32[]{:S(2)}, u32[]{:S(2)}) async-start(bf16[4,640,64]{1,2,0:T(8,128)(2,1)} %bitcast.15), calls=%async_computation | async-start | bytes 655360 | tf_op jit(solution)/shard_map/all_to_all | solution.py:432
  630.2 6.3 copy-start.2
Sparse Core Ops, SparseCore 0:
  10.0 26.2 all-gather.8
  38.8 32.2 all-gather.6
  73.5 36.7 all-gather.10
  112.6 36.7 all-gather.12
  266.7 33.6 reduce-scatter.11
  304.3 36.0 reduce-scatter.15
  344.1 46.2 reduce-scatter.13
  393.8 51.3 reduce-scatter.19
  448.9 51.3 reduce-scatter.17
  503.7 33.6 reduce-scatter.23
  540.2 19.0 reduce-scatter.21
  561.8 68.3 all-reduce.4

commit v2 on v1

--- a/solution.py
+++ b/solution.py
@@ -110,13 +110,172 @@
     return jnp.concatenate([part, zero] if e == 0 else [zero, part], axis=0)
 
 
-def step_kernel(
-    tok_ref, tgt_ref, val_ref, table_ref, gm_ref, gf_ref, gz_ref, wm_ref, wo_ref, we_ref, wr_ref,
-    loss_ref, lg_ref, dtable_ref, dgm_ref, dgf_ref, dgz_ref, dwm_ref, dwo_ref, dwe_ref, dwrt_ref,
-    x_ref, x1_ref, dx_ref, kv_ref, pT_ref, kf_ref, inv1_ref, cum_ref, oT_ref, hT_ref, g_ref, gT_ref,
-    wide_ref, a1k_ref, m_ref, d_ref, ds_ref, doT_ref, do_ref, dpT_ref, part_ref, w_ref, yb_ref, acc_ref,
-    stage_ref, sem_ref,
+class Links:
+    def __init__(self, pieces, send_sem, recv_sem):
+        self.pieces, self.send_sem, self.recv_sem = pieces, send_sem, recv_sem
+        d = lax.axis_index("dp")
+        core, x, y = d % 2, (d // 2) % 2, d // 4
+        self.d = d
+        self.core_n, self.x_n, self.y_n = d + 1 - 2 * core, d + 2 - 4 * x, d + 4 - 8 * y
+        self.diag = self.x_n + 4 - 8 * y
+
+    def copy(self, n, kind):
+        ref, rows, split = self.pieces[n]
+        d, core_n, x_n, y_n, diag = self.d, self.core_n, self.x_n, self.y_n, self.diag
+        block = (d, d, y_n, x_n, d, x_n, y_n, diag, diag)[kind]
+        target = (x_n, y_n, x_n, y_n, core_n, core_n, core_n, core_n, core_n)[kind]
+        view = ref.at[pl.ds(pl.multiple_of(block * rows, rows), rows)]
+        if kind in (2, 7):
+            view = view.at[:, :split]
+        if kind in (3, 8):
+            view = view.at[:, split:]
+        return pltpu.make_async_remote_copy(
+            src_ref=view, dst_ref=view, send_sem=self.send_sem.at[n, kind], recv_sem=self.recv_sem.at[n, kind],
+            device_id={"dp": target}, device_id_type=pl.DeviceIdType.MESH,
+        )
+
+    def own(self, *ns):
+        for n in ns:
+            for kind in (0, 1, 4):
+                self.copy(n, kind).start()
+
+    def first(self, *ns):
+        for n in ns:
+            self.copy(n, 0).wait_recv()
+            self.copy(n, 3).start()
+            self.copy(n, 1).wait_recv()
+            self.copy(n, 2).start()
+            self.copy(n, 5).start()
+            self.copy(n, 6).start()
+
+    def second(self, *ns):
+        for n in ns:
+            self.copy(n, 2).wait_recv()
+            self.copy(n, 7).start()
+            self.copy(n, 3).wait_recv()
+            self.copy(n, 8).start()
+
+    def ready(self, *ns):
+        for n in ns:
+            for kind in (4, 5, 6, 7, 8):
+                self.copy(n, kind).wait_recv()
+
+    def finish(self):
+        for n in range(len(self.pieces)):
+            for kind in range(9):
+                self.copy(n, kind).wait_send()
+
+
+def step_kernel(linked, *refs):
+    names = (LINKED_IN if linked else PLAIN_IN) + (LINKED_OUT if linked else PLAIN_OUT)
+    names += tuple(SCRATCH) + (tuple(LINKED_SCRATCH) if linked else ())
+    step_body(linked, **dict(zip(names, refs, strict=True)))
+
+
+def step_body(
+    linked, tok, tgt, val, loss, lg, dtable, dgm, dgf, dgz, dwm, dwo, dwe, dwrt,
+    x, x1, dx, kv, pT, kf, inv1s, cum, oT, hT, g, gT, wide, a1k, m, d, ds, doT, do, dpT, part, w, yb, acc, stage, sem,
+    table=None, gm=None, gf=None, gz=None, wm=None, wo=None, we=None, wr=None,
+    small=None, wm_s=None, wo_s=None, we_s=None, wr_s=None, tz=None, gains=None, lgs=None, losss=None,
+    send_sem=None, recv_sem=None, zsend=None, zrecv=None,
 ):
+    tok_ref, tgt_ref, val_ref, table_ref = tok, tgt, val, table
+    gm_ref, gf_ref, gz_ref = gm, gf, gz
+    wm_ref, wo_ref, we_ref, wr_ref = wm, wo, we, wr
+    loss_ref, lg_ref, dtable_ref, dgm_ref, dgf_ref, dgz_ref = loss, lg, dtable, dgm, dgf, dgz
+    dwm_ref, dwo_ref, dwe_ref, dwrt_ref = dwm, dwo, dwe, dwrt
+    x_ref, x1_ref, dx_ref, kv_ref, pT_ref, kf_ref, inv1_ref, cum_ref = x, x1, dx, kv, pT, kf, inv1s, cum
+    oT_ref, hT_ref, g_ref, gT_ref, wide_ref, a1k_ref, m_ref, d_ref, ds_ref = oT, hT, g, gT, wide, a1k, m, d, ds
+    doT_ref, do_ref, dpT_ref, part_ref, w_ref, yb_ref, acc_ref = doT, do, dpT, part, w, yb, acc
+    stage_ref, sem_ref = stage, sem
+    r, c = iotas(LEN, LEN)
+    upper = (r <= c).astype(F32).astype(BF16)
+
+    if linked:
+        zi = lax.axis_index("section")
+        links = Links(
+            [(table_ref, 64, 256)]
+            + [
+                entry
+                for l in range(LAYERS)
+                for entry in (
+                    (wm_ref.at[l], 64, 3 * D // 2),
+                    (wo_ref.at[l], 64, D // 2),
+                    (we_ref.at[l], 64, FF // 2),
+                    (wr_ref.at[l], 256, D // 2),
+                )
+            ],
+            send_sem, recv_sem,
+        )
+
+        def along_z(n, k, src_of, dst):
+            target = (zi + k) % 4
+            return pltpu.make_async_remote_copy(
+                src_ref=src_of(target), dst_ref=dst.at[zi], send_sem=zsend.at[n, k - 1], recv_sem=zrecv.at[n, k - 1],
+                device_id={"section": target}, device_id_type=pl.DeviceIdType.MESH,
+            )
+
+        def table_copy(k):
+            return along_z(0, k, lambda target: tz.at[zi], tz)
+
+        def lg_copy(k):
+            return along_z(1, k, lambda target: lgs.at[target], lg_ref)
+
+        def loss_copy(k):
+            return along_z(2, k, lambda target: losss, loss_ref)
+
+        barrier = pltpu.get_barrier_semaphore()
+        for target in (links.core_n, links.x_n, links.y_n):
+            pl.semaphore_signal(barrier, inc=1, device_id={"dp": target}, device_id_type=pl.DeviceIdType.MESH)
+        for k in (1, 2, 3):
+            pl.semaphore_signal(barrier, inc=1, device_id={"section": (zi + k) % 4}, device_id_type=pl.DeviceIdType.MESH)
+        pl.semaphore_wait(barrier, 6)
+
+        own64 = pl.ds(pl.multiple_of(links.d * 64, 64), 64)
+        own256 = pl.ds(pl.multiple_of(links.d * 256, 256), 256)
+        small_b = small[...].astype(BF16)
+        tz[zi] = small_b
+        for k in (1, 2, 3):
+            table_copy(k).start()
+        wm_ref[0, own64] = wm_s[0].astype(BF16)
+        links.own(1)
+        wo_ref[0, own64] = wo_s[0].astype(BF16)
+        we_ref[0, own64] = we_s[0].astype(BF16)
+        wr_ref[0, own256] = wr_s[0].astype(BF16)
+        for k in (1, 2, 3):
+            table_copy(k).wait_recv()
+        pad = jnp.zeros((64, 64), BF16)
+        table_ref[own64, :] = jnp.concatenate([tz[i][:, :64] for i in range(4)] + [small_b[:, 64:], pad], axis=1)
+        links.own(0, 2, 3)
+        wide_ref[...] = upper
+        wm_ref[1, own64] = wm_s[1].astype(BF16)
+        wo_ref[1, own64] = wo_s[1].astype(BF16)
+        we_ref[1, own64] = we_s[1].astype(BF16)
+        wr_ref[1, own256] = wr_s[1].astype(BF16)
+        links.first(1, 0)
+        links.second(1, 0)
+        links.own(4)
+        links.ready(0)
+        gains[...] = table_ref[:, 256:].astype(F32).T
+        table_ref = table_ref.at[:, :256]
+        gm_ref, gf_ref, gz_ref = [gains[i:i + 1] for i in range(2)], [gains[i:i + 1] for i in range(2, 4)], gains[4:5]
+        links.ready(1)
+    else:
+        wide_ref[...] = upper
+        gm_ref, gf_ref, gz_ref = [gm_ref[i] for i in range(2)], [gf_ref[i] for i in range(2)], gz_ref[...]
+
+    def service(step, index=None):
+        if not linked:
+            return
+        for at, act in SERVICE.get(step, {}).items():
+            def run(act=act):
+                for name, ns in act:
+                    getattr(links, name)(*ns)
+            if at is None:
+                run()
+            else:
+                pl.when(index == at)(run)
+
     inv2 = 1.0 / (lax.broadcasted_iota(jnp.int32, (1, LEN), 1).astype(F32) + 1.0)
 
     def emit(slot, wait_first, value, dst):
@@ -133,9 +292,6 @@
     vocab_ids = lax.broadcasted_iota(jnp.int32, (LEN, VOCAB), 1)
     hot = (vocab_ids == tok_ref[...]).astype(F32).astype(BF16)
     x_ref[0] = mm_nt(hot, table_ref[...])
-    r, c = iotas(LEN, LEN)
-    upper = (r <= c).astype(F32).astype(BF16)
-    wide_ref[...] = upper
 
     def attention_forward(l):
         x = x_ref[l]
@@ -146,6 +302,7 @@
             if j > 0:
                 kv_ref[l, :, (j - 1) * TILE:j * TILE] = part
             pT_ref[l, j * TILE:(j + 1) * TILE, :] = part.T
+        service(("mixer", l))
         kT = pT_ref[l, D:2 * D, :].astype(F32)
         a1k_ref[...] = feature_parts(kT)[0].astype(BF16)
         for i in range(CHUNKS):
@@ -174,9 +331,11 @@
                     t0, t1 = i * CH, (i + 1) * CH
                     mixture, _ = mixture_chunk(i, key_nat, key_feat2, query_masked, query_feat2)
                     oT_ref[l, pl.ds(row, HD), t0:t1] = mm(vT[:, :t1], mixture).astype(BF16)
+            service(("pair", l), p)
             return carry
 
         lax.fori_loop(0, HEADS // 2, pair, 0)
+        service(("output", l))
         o = oT_ref[l].T
         x1_ref[l] = x_ref[l] + mm(o, wo_ref[l])
 
@@ -185,18 +344,20 @@
         g_ref[l] = norm_forward(x1, gf_ref[l]).astype(BF16)
         gT_ref[l] = g_ref[l].T
         x_ref[l + 1] = x1
+        service(("feed", l))
 
         def tile(j, carry):
             col = pl.multiple_of(j * TILE, TILE)
             active = gelu_parts(mm(g_ref[l], we_ref[l, :, pl.ds(col, TILE)]))[0].astype(BF16)
             x_ref[l + 1] += mm(active, wr_ref[l, pl.ds(col, TILE), :])
+            service(("tile", l), j)
             return carry
 
         lax.fori_loop(0, FF // TILE, tile, 0)
 
     def head():
         x = x_ref[LAYERS]
-        z = norm_forward(x, gz_ref[...]).astype(BF16)
+        z = norm_forward(x, gz_ref).astype(BF16)
         logits = mm(z, table_ref[...])
         tgt_hot = (vocab_ids == tgt_ref[...]).astype(F32)
         val = val_ref[...]
@@ -207,11 +368,22 @@
         picked = jnp.sum(logits * tgt_hot, axis=-1, keepdims=True)
         cross = (lse - picked) * val
         loss = jnp.sum(cross, axis=0, keepdims=True) / jnp.sum(val, axis=0, keepdims=True)
-        loss_ref[...] = jnp.broadcast_to(loss, loss_ref.shape)
+        loss = jnp.broadcast_to(loss, (8, 128))
         grad_b = ((grown / total - tgt_hot) * val).astype(BF16)
-        lg_ref[...] = grad_b
+        if linked:
+            losss[...] = loss
+            for i in range(4):
+                lgs[i] = grad_b[:, 64 * i:64 * i + 64]
+            for k in (1, 2, 3):
+                lg_copy(k).start()
+                loss_copy(k).start()
+            pltpu.make_async_copy(lgs.at[zi], lg_ref.at[zi], zsend.at[1, 3]).start()
+            pltpu.make_async_copy(losss, loss_ref.at[zi], zsend.at[2, 3]).start()
+        else:
+            loss_ref[...] = loss
+            lg_ref[...] = grad_b
         dtable_ref[...] = mm(z.T, grad_b)
-        dv, dgain = norm_backward(x, gz_ref[...], mm_nt(grad_b, table_ref[...]))
+        dv, dgain = norm_backward(x, gz_ref, mm_nt(grad_b, table_ref[...]))
         dgz_ref[...] = dgain
         dx_ref[...] = dv
 
@@ -326,6 +498,7 @@
         dx_ref[...] += dv
 
     for l in range(LAYERS):
+        service(("layer", l))
         attention_forward(l)
         feed_forward(l)
     head()
@@ -335,17 +508,94 @@
     dtable_ref[...] += mm(dx_ref[...].astype(BF16).T, hot)
     for slot in range(4):
         pltpu.make_async_copy(stage_ref.at[slot], dwo_ref.at[0], sem_ref.at[slot]).wait()
-
-
-def local_step(tok, tgt, val, table, gm, gf, gz, wm, wo, we, wr):
+    if linked:
+        pltpu.make_async_copy(lgs.at[zi], lg_ref.at[zi], zsend.at[1, 3]).wait()
+        pltpu.make_async_copy(losss, loss_ref.at[zi], zsend.at[2, 3]).wait()
+        for k in (1, 2, 3):
+            table_copy(k).wait_send()
+            lg_copy(k).wait()
+            loss_copy(k).wait()
+        links.finish()
+
+
+SERVICE = {
+    ("mixer", 0): {None: (("first", (2, 3)), ("own", (5,)))},
+    ("pair", 0): {
+        0: (("second", (2, 3)),),
+        1: (("first", (4,)), ("own", (6, 7))),
+        2: (("second", (4,)), ("ready", (2, 3))),
+        3: (("first", (5,)),),
+    },
+    ("feed", 0): {None: (("ready", (4,)), ("second", (5,)), ("own", (8,)))},
+    ("tile", 0): {1: (("first", (6, 7)),), 2: (("second", (6,)),), 3: (("second", (7,)),)},
+    ("layer", 1): {None: (("ready", (5,)),)},
+    ("mixer", 1): {None: (("first", (8,)),)},
+    ("pair", 1): {1: (("second", (8,)),)},
+    ("output", 1): {None: (("ready", (6,)),)},
+    ("feed", 1): {None: (("ready", (7, 8)),)},
+}
+PLAIN_IN = ("tok", "tgt", "val", "table", "gm", "gf", "gz", "wm", "wo", "we", "wr")
+PLAIN_OUT = ("loss", "lg", "dtable", "dgm", "dgf", "dgz", "dwm", "dwo", "dwe", "dwrt")
+LINKED_IN = ("tok", "tgt", "val", "small", "wm_s", "wo_s", "we_s", "wr_s")
+LINKED_OUT = PLAIN_OUT
+SCRATCH = dict(
+    x=pltpu.VMEM((LAYERS + 1, LEN, D), F32),
+    x1=pltpu.VMEM((LAYERS, LEN, D), F32),
+    dx=pltpu.VMEM((LEN, D), F32),
+    kv=pltpu.VMEM((LAYERS, LEN, 2 * D), BF16),
+    pT=pltpu.VMEM((LAYERS, 3 * D, LEN), BF16),
+    kf=pltpu.VMEM((LAYERS, LEN, 2 * D), BF16),
+    inv1s=pltpu.VMEM((LAYERS, HEADS, 1, LEN), F32),
+    cum=pltpu.VMEM((LAYERS, D, LEN), F32),
+    oT=pltpu.VMEM((LAYERS, D, LEN), BF16),
+    hT=pltpu.VMEM((LAYERS, D, LEN), BF16),
+    g=pltpu.VMEM((LAYERS, LEN, D), BF16),
+    gT=pltpu.VMEM((LAYERS, D, LEN), BF16),
+    wide=pltpu.VMEM((LEN, LEN), BF16),
+    a1k=pltpu.VMEM((D, LEN), BF16),
+    m=pltpu.VMEM((2, LEN, LEN), BF16),
+    d=pltpu.VMEM((2, LEN, LEN), BF16),
+    ds=pltpu.VMEM((2, LEN, 2 * CH), BF16),
+    doT=pltpu.VMEM((D, LEN), BF16),
+    do=pltpu.VMEM((LEN, D), BF16),
+    dpT=pltpu.VMEM((3 * D, LEN), BF16),
+    part=pltpu.VMEM((D, LEN), F32),
+    w=pltpu.VMEM((D, LEN), BF16),
+    yb=pltpu.VMEM((LEN, D), BF16),
+    acc=pltpu.VMEM((LEN, D), F32),
+    stage=pltpu.VMEM((4, D, TILE), BF16),
+    sem=pltpu.SemaphoreType.DMA((4,)),
+)
+LINKED_SCRATCH = dict(
+    table=pltpu.VMEM((D, 384), BF16),
+    wm=pltpu.VMEM((LAYERS, D, 3 * D), BF16),
+    wo=pltpu.VMEM((LAYERS, D, D), BF16),
+    we=pltpu.VMEM((LAYERS, D, FF), BF16),
+    wr=pltpu.VMEM((LAYERS, FF, D), BF16),
+    tz=pltpu.VMEM((4, 64, 128), BF16),
+    gains=pltpu.VMEM((128, D), F32),
+    lgs=pltpu.VMEM((4, LEN, 64), BF16),
+    losss=pltpu.VMEM((8, 128), F32),
+    send_sem=pltpu.SemaphoreType.DMA((9, 9)),
+    recv_sem=pltpu.SemaphoreType.DMA((9, 9)),
+    zsend=pltpu.SemaphoreType.DMA((3, 4)),
+    zrecv=pltpu.SemaphoreType.DMA((3, 4)),
+)
+
+
+def local_step(linked, *operands):
     vmem = pl.BlockSpec(memory_space=pltpu.VMEM)
     hbm = pl.BlockSpec(memory_space=pl.ANY)
     shape = jax.ShapeDtypeStruct
+    scratch = dict(SCRATCH, **LINKED_SCRATCH) if linked else SCRATCH
+    if linked:
+        first_out = (shape((4, 8, 128), F32), shape((4, LEN, 64), BF16))
+    else:
+        first_out = (shape((8, 128), F32), shape((LEN, VOCAB), BF16))
     return pl.pallas_call(
-        step_kernel,
-        out_shape=(
-            shape((8, 128), F32),
-            shape((LEN, VOCAB), BF16),
+        functools.partial(step_kernel, linked),
+        out_shape=first_out
+        + (
             shape((D, VOCAB), F32),
             shape((LAYERS, 1, D), F32),
             shape((LAYERS, 1, D), F32),
@@ -355,40 +605,17 @@
             shape((LAYERS, D, FF), BF16),
             shape((LAYERS, D, FF), BF16),
         ),
-        in_specs=[vmem] * 11,
-        out_specs=(vmem,) * 6 + (hbm,) * 4,
-        scratch_shapes=[
-            pltpu.VMEM((LAYERS + 1, LEN, D), F32),
-            pltpu.VMEM((LAYERS, LEN, D), F32),
-            pltpu.VMEM((LEN, D), F32),
-            pltpu.VMEM((LAYERS, LEN, 2 * D), BF16),
-            pltpu.VMEM((LAYERS, 3 * D, LEN), BF16),
-            pltpu.VMEM((LAYERS, LEN, 2 * D), BF16),
-            pltpu.VMEM((LAYERS, HEADS, 1, LEN), F32),
-            pltpu.VMEM((LAYERS, D, LEN), F32),
-            pltpu.VMEM((LAYERS, D, LEN), BF16),
-            pltpu.VMEM((LAYERS, D, LEN), BF16),
-            pltpu.VMEM((LAYERS, LEN, D), BF16),
-            pltpu.VMEM((LAYERS, D, LEN), BF16),
-            pltpu.VMEM((LEN, LEN), BF16),
-            pltpu.VMEM((D, LEN), BF16),
-            pltpu.VMEM((2, LEN, LEN), BF16),
-            pltpu.VMEM((2, LEN, LEN), BF16),
-            pltpu.VMEM((2, LEN, 2 * CH), BF16),
-            pltpu.VMEM((D, LEN), BF16),
-            pltpu.VMEM((LEN, D), BF16),
-            pltpu.VMEM((3 * D, LEN), BF16),
-            pltpu.VMEM((D, LEN), F32),
-            pltpu.VMEM((D, LEN), BF16),
-            pltpu.VMEM((LEN, D), BF16),
-            pltpu.VMEM((LEN, D), F32),
-            pltpu.VMEM((4, D, TILE), BF16),
-            pltpu.SemaphoreType.DMA((4,)),
-        ],
-        compiler_params=pltpu.CompilerParams(vmem_limit_bytes=63 * 1024 * 1024),
+        in_specs=[vmem] * len(operands),
+        out_specs=(hbm if linked else vmem,) * 2 + (vmem,) * 4 + (hbm,) * 4,
+        scratch_shapes=list(scratch.values()),
+        compiler_params=pltpu.CompilerParams(
+            vmem_limit_bytes=63 * 1024 * 1024,
+            collective_id=0 if linked else None,
+            has_side_effects=linked,
+        ),
         cost_estimate=pl.CostEstimate(flops=40_000_000_000, bytes_accessed=40_000_000, transcendentals=0),
         name="local_step",
-    )(tok, tgt, val, table, gm, gf, gz, wm, wo, we, wr)
+    )(*operands)
 
 
 def body(
@@ -414,22 +641,31 @@
     target_row = jnp.concatenate([token_row[1:], jnp.zeros((1,), jnp.int32)])
     valid_row = jnp.concatenate([mask_row[1:], jnp.zeros((1,), jnp.int32)]).astype(F32)
 
-    def gather(block, dim):
-        return lax.all_gather(block.astype(BF16), "dp", axis=dim, tiled=True)
-
-    table = lax.all_gather(gather(embedding, 0), "section", axis=1, tiled=True)
-    gains = gather(jnp.concatenate([mixer_gain, feed_gain, final_gain[None]], axis=0), 1).astype(F32)
-    wm = gather(mixer_weight, 1)
-    wo = gather(output_weight, 1)
-    we = gather(expand_weight, 1)
-    wr = gather(reduce_weight, 1)
-    loss, lg, dtable, dgm, dgf, dgz, dwm, dwo, dwe, dwrt = local_step(
-        token_row[:, None], target_row[:, None], valid_row[:, None], table,
-        gains[0:2, None], gains[2:4, None], gains[4:5], wm, wo, we, wr,
-    )
-    item_loss = lax.all_gather(loss[0, 0], "section")
-    parts = lg.reshape(LEN, segments, slice_width).transpose(1, 0, 2)
-    logit_grad = lax.all_to_all(parts, "section", 0, 0, tiled=True).astype(F32)
+    columns = (token_row[:, None], target_row[:, None], valid_row[:, None])
+    linked = segments == 4 and lax.axis_size("dp") == 8
+    if linked:
+        small = jnp.concatenate(
+            [embedding, mixer_gain.T, feed_gain.T, final_gain[:, None], jnp.zeros((embedding.shape[0], 59), F32)], axis=1
+        )
+        loss, lg, dtable, dgm, dgf, dgz, dwm, dwo, dwe, dwrt = local_step(
+            True, *columns, small, mixer_weight, output_weight, expand_weight, reduce_weight
+        )
+        item_loss = loss[:, 0, 0]
+        logit_grad = lg.astype(F32)
+    else:
+
+        def gather(block, dim):
+            return lax.all_gather(block.astype(BF16), "dp", axis=dim, tiled=True)
+
+        table = lax.all_gather(gather(embedding, 0), "section", axis=1, tiled=True)
+        gains = gather(jnp.concatenate([mixer_gain, feed_gain, final_gain[None]], axis=0), 1).astype(F32)
+        loss, lg, dtable, dgm, dgf, dgz, dwm, dwo, dwe, dwrt = local_step(
+            False, *columns, table, gains[0:2, None], gains[2:4, None], gains[4:5],
+            gather(mixer_weight, 1), gather(output_weight, 1), gather(expand_weight, 1), gather(reduce_weight, 1),
+        )
+        item_loss = lax.all_gather(loss[0, 0], "section")
+        parts = lg.reshape(LEN, segments, slice_width).transpose(1, 0, 2)
+        logit_grad = lax.all_to_all(parts, "section", 0, 0, tiled=True).astype(F32)
 
     def shard(grad, dim):
         part = lax.psum_scatter(grad.astype(BF16), "dp", scatter_dimension=dim, tiled=True)

time: 649 us -> 552 us (0.85)
  waiting for transfers between devices: 431 us -> 340 us
  Pallas kernels: 115 us -> 155 us
  blocking collectives: 46 us -> 11.7 us
  other arithmetic: 14.9 us -> 8.27 us
    all_gather x4 -> x0, waiting for transfers between devices: 95 us -> none  [gather(): return lax.all_gather(block.astype(BF16), 'dp', axis=dim, tiled=True)]
    all_gather x4 -> x0, blocking collectives: 46 us -> none  [the longest x2 19.5 us: gather(): return lax.all_gather(block.astype(BF16), 'dp', axis=dim, tiled=True)]
    pallas_call x1, Pallas kernels: 115 us -> 155 us  [local_step(): pl.pallas_call(functools.partial(step_kernel, linked), out_shape=first_ou...]
    psum x0 -> x1, blocking collectives: none -> 11.7 us  [body(): gain_grads = lax.psum(gain_grads, 'section')]
    convert_element_type x7 -> x0, other arithmetic: 7.44 us -> none  [the longest x5 6.55 us: gather(): return lax.all_gather(block.astype(BF16), 'dp', axis=dim, tiled=True)]
    unnamed x14 -> x10, waiting for transfers between devices: 38.9 us -> 45.5 us
  transfers between devices with their start and end apart: 13 -> 8, of which waited for: 11 -> 8; matrix products, arithmetic and copies ran while one was open for 3% -> 1% of each run, Pallas kernels for 0% -> 0%
where the time goes in v2:
time: 552 us; the launch traced here: 548 us
  waiting for transfers between devices  340 us (62%)
  Pallas kernels  155 us (28%)
  local copies, waits for them, and re-layouts  17.7 us (3%)
  between operations  14.7 us (3%)
  blocking collectives  11.7 us (2%)
  other arithmetic  8.27 us (1%)
    reduce_scatter x4, waiting for transfers between devices, shard(): lax.psum_scatter(grad.astype(BF16), 'dp', scatter_dimension=dim, tiled=True)  198 us
    pallas_call x1, Pallas kernels, local_step(): pl.pallas_call(functools.partial(step_kernel, linked), out_shape=first_ou...  155 us
    psum x1, waiting for transfers between devices, shard(): return lax.psum(part, 'section').astype(F32)  69.6 us
    unnamed x10, waiting for transfers between devices  45.5 us
    reduce_scatter x1, waiting for transfers between devices, body(): lax.psum_scatter(dtable.astype(BF16), 'dp', scatter_dimension=0, tiled=True)  27.3 us
    psum x1, blocking collectives, body(): gain_grads = lax.psum(gain_grads, 'section')  11.7 us
  transfers between devices with their start and end apart: 8, of which 8 were waited for; matrix products, arithmetic and copies ran while one was open for 1% of the time, Pallas kernels for 0%

profile of v2, /device:TPU:0, one launch (start us, length us, event | category | flops | bytes accessed | tf_op | source)
XLA Modules:
  0.0 548.0 jit_solution(5454901124620739494)
XLA Ops:
  7.2 0.0 reduce-scatter.12.cloned.1.call-start
  7.2 0.8 copy.41
  8.0 0.8 copy.42
  8.8 0.7 copy.43
  9.5 0.7 dynamic-slice_bitcast_fusion.1
  10.2 0.8 dynamic-slice_bitcast_fusion
  11.0 0.1 pad_add_fusion
  11.1 0.9 broadcast_in_dim.17.refs_1_
  12.0 0.1 add_convert_fusion
  12.1 0.9 copy.46.refs_2_
  13.0 0.9 copy.44.refs_0_
  13.9 1.5 concatenate.24.refs_3_
  15.3 155.4 %local_step.1 = (f32[4,8,128]{2,1,0:T(8,128)}, bf16[4,640,64]{2,1,0:T(8,128)(2,1)}, f32[512,256]{1,0:T(8,128)}, f32[2,1,512]{2,1,0:T(1,128)}, f32[2,1,512]{2,1,0...) custom-call(s32[640,1]{1,0:T(8,128)} %copy.44.refs_0_, ...), custom_call_target="tpu_custom_call" | custom-call | flops 40000000000 | bytes 40000000 | tf_op jit(solution)/shard_map/local_step/pallas_call | solution.py:595
  170.8 1.8 convert_element_type.31
  172.6 0.0 reduce-scatter.12.cloned.1.call-update
  172.6 0.0 reduce-scatter.16.cloned.1.call-start
  172.6 0.7 reduce-scatter.16.cloned.1.call-update
  173.3 0.0 reduce-scatter.14.cloned.1.call-start
  173.4 0.7 reduce-scatter.14.cloned.1.call-update
  174.1 0.0 reduce-scatter.18.cloned.1.call-start
  174.1 0.0 copy-start.2
  174.1 0.0 copy-start.1
  174.1 0.0 copy-start.3
  174.2 0.5 reduce-scatter.18.cloned.1.call-update
  174.7 0.0 copy-start
  174.7 0.0 reduce-scatter.20.cloned.1.call-start
  174.7 0.5 reduce-scatter.20.cloned.1.call-update
  175.2 0.0 reduce-scatter.24.cloned.1.call-start
  175.3 0.0 copy-done.2
  175.3 0.0 copy-done.1
  175.3 0.0 copy-done.3
  175.4 0.9 copy.51
  176.2 0.0 reduce-scatter.24.cloned.1.call-update
  176.3 0.0 reduce-scatter.22.cloned.1.call-start
  176.3 27.3 %reduce-scatter.12.cloned.1.call-done = bf16[64,256]{1,0:T(8,128)(2,1)} async-done(((bf16[512,256]{1,0:T(8,128)(2,1)}), bf16[64,256]{1,0:T(8,128)(2,1)}) %reduce-scatter.12.cloned.1.call-update) | async-done | bytes 32784 | tf_op jit(solution)/shard_map/reduce_scatter | solution.py:674
  203.6 1.5 copy.49
  205.1 0.0 reduce-scatter.22.cloned.1.call-update
  205.1 0.0 all-reduce.3.cloned.1.call-start
  205.2 38.0 %reduce-scatter.16.cloned.1.call-done = bf16[2,64,512]{2,1,0:T(8,128)(2,1)} async-done(((bf16[2,512,512]{2,1,0:T(8,128)(2,1)}), bf16[2,64,512]{2,1,0:T(8,128)(2,1)}) %reduce-scatter.16.cloned.1.call-update) | async-done | bytes 131088 | tf_op jit(solution)/shard_map/reduce_scatter | solution.py:671
  243.1 50.0 %reduce-scatter.14.cloned.1.call-done = bf16[2,64,1536]{2,1,0:T(8,128)(2,1)} async-done(((bf16[2,512,1536]{2,1,0:T(8,128)(2,1)}), bf16[2,64,1536]{2,1,0:T(8,128)(2,1)}) %reduce-scatter.14.cloned.1.call-update) | async-done | bytes 393232 | tf_op jit(solution)/shard_map/reduce_scatter | solution.py:671
  293.2 54.6 %reduce-scatter.18.cloned.1.call-done = bf16[2,64,2048]{2,1,0:T(8,128)(2,1)} async-done(((bf16[2,512,2048]{2,1,0:T(8,128)(2,1)}), bf16[2,64,2048]{2,1,0:T(8,128)(2,1)}) %reduce-scatter.18.cloned.1.call-update) | async-done | bytes 524304 | tf_op jit(solution)/shard_map/reduce_scatter | solution.py:671
  347.8 54.9 %reduce-scatter.20.cloned.1.call-done = bf16[2,512,256]{2,1,0:T(8,128)(2,1)} async-done(((bf16[2,512,2048]{2,1,0:T(8,128)(2,1)}), bf16[2,512,256]{2,1,0:T(8,128)(2,1)}) %reduce-scatter.20.cloned.1.call-update) | async-done | bytes 524304 | tf_op jit(solution)/shard_map/reduce_scatter | solution.py:671
  402.7 0.0 all-reduce.3.cloned.1.call-update
  402.7 0.0 copy-done
  402.7 1.1 copy.47
  403.8 1.3 slice_reduce_fusion
  405.1 34.6 %reduce-scatter.24.cloned.1.call-done = f32[64,5]{1,0:T(8,128)} async-done(((f32[512,5]{1,0:T(8,128)}), f32[64,5]{1,0:T(8,128)}) %reduce-scatter.24.cloned.1.call-update) | async-done | bytes 1296
  439.8 0.8 copy.52
  440.6 11.7 %psum.37 = f32[5,64]{1,0:T(8,128)S(1)} all-reduce(f32[5,64]{1,0:T(8,128)S(1)} %copy.52), channel_id=1, replica_groups=mesh['section'=4,'dp'=8] {'section'}, use_global_device_ids=true, to_apply=%region_7.8 | all-reduce | flops 320 | bytes 2560 | tf_op jit(solution)/shard_map/psum | solution.py:679
  452.3 0.5 slice_bitcast_fusion
  452.8 0.6 fusion
  453.4 8.4 %reduce-scatter.22.cloned.1.call-done = bf16[64,64]{1,0:T(8,128)(2,1)} async-done(((bf16[256,64]{1,0:T(8,128)(2,1)}), bf16[64,64]{1,0:T(8,128)(2,1)}) %reduce-scatter.22.cloned.1.call-update) | async-done | bytes 8208
  461.7 0.8 copy.50
  462.5 0.6 convert_element_type.32
  463.2 69.6 %all-reduce.3.cloned.1.call-done = (bf16[2,256,512]{1,2,0:T(8,128)(2,1)}, bf16[2,64,1536]{2,1,0:T(8,128)(2,1)}, bf16[2,64,512]{2,1,0:T(8,128)(2,1)}, bf16[2,64,2048]{2,1,0:T(8,128)(2,1)}) async-done(((bf16[2,256,512]{1,2,0:T(8,128)(2,1)}, bf16[2,64,1536]{2,1,0:T(8,128)(2,1)}, bf16[2,64,512]{2,1,0:T(8,128)(2,1)}, bf16[2,64,2048]{2,1,0:T(8,128)(2,1)}), (bf16[2,256,512]{1,2,0:T(8,128)(2,1)}, ...) | async-done | bytes 1572880 | tf_op jit(solution)/shard_map/psum | solution.py:672
  532.8 1.6 convert_element_type.34
  534.4 2.2 copy.48
  536.6 2.0 convert_element_type.33
  538.6 2.1 convert_element_type.35
  (4 shorter events, 0.0 us)
Async XLA Ops:
  7.2 196.4 %reduce-scatter.12.cloned.1.call-start = ((), (), s32[]{:S(2)}) async-start(), calls=%async_computation.7 | async-start | bytes 294912 | tf_op jit(solution)/shard_map/reduce_scatter | solution.py:674
  172.6 70.6 %reduce-scatter.16.cloned.1.call-start = ((), (), s32[]{:S(2)}) async-start(), calls=%async_computation.9 | async-start | bytes 1179648 | tf_op jit(solution)/shard_map/reduce_scatter | solution.py:671
  173.3 119.8 %reduce-scatter.14.cloned.1.call-start = ((), (), s32[]{:S(2)}) async-start(), calls=%async_computation.8 | async-start | bytes 3538944 | tf_op jit(solution)/shard_map/reduce_scatter | solution.py:671
  174.1 173.7 %reduce-scatter.18.cloned.1.call-start = ((), (), s32[]{:S(2)}) async-start(), calls=%async_computation.10 | async-start | bytes 4718592 | tf_op jit(solution)/shard_map/reduce_scatter | solution.py:671
  174.1 1.2 copy-start.2
  174.1 1.2 copy-start.1
  174.1 1.2 copy-start.3
  174.7 228.1 %copy-start = (bf16[4,640,64]{2,1,0:T(8,128)(2,1)S(1)}, bf16[4,640,64]{2,1,0:T(8,128)(2,1)}, u32[]{:S(2)}) copy-start(bf16[4,640,64]{2,1,0:T(8,128)(2,1)} %get-tuple-element.21) | copy-start | bytes 983044
  174.7 228.0 %reduce-scatter.20.cloned.1.call-start = ((), (), s32[]{:S(2)}) async-start(), calls=%async_computation.11 | async-start | bytes 4718592 | tf_op jit(solution)/shard_map/reduce_scatter | solution.py:671
  175.2 264.5 %reduce-scatter.24.cloned.1.call-start = ((), (), s32[]{:S(2)}) async-start(), calls=%async_computation.13 | async-start | bytes 294912
  176.3 285.5 %reduce-scatter.22.cloned.1.call-start = ((), (), s32[]{:S(2)}) async-start(), calls=%async_computation.12 | async-start | bytes 81920
  205.1 327.7 %all-reduce.3.cloned.1.call-start = ((), (), s32[]{:S(2)}) async-start(), calls=%async_computation.14 | async-start | bytes 3145728 | tf_op jit(solution)/shard_map/psum | solution.py:672
Sparse Core Ops, SparseCore 0:
  172.7 30.8 reduce-scatter.11
  207.1 36.0 reduce-scatter.15
  246.9 46.2 reduce-scatter.13
  296.4 51.3 reduce-scatter.17
  351.3 51.3 reduce-scatter.19
  406.1 33.5 reduce-scatter.23
  442.7 19.0 reduce-scatter.21
  464.3 68.3 all-reduce.2
